TPU v7x, 32 devices: a whole 2x2x4 slice. The times are simulated.
32 devices in a mesh: rep: 2 (over x), seq: 16 (over z, y, core).
Axes of the slice: x: 2, y: 2, z: 4, core: 2. Of those that a mesh axis runs over, the one named last changes fastest.
Arguments:
- cached_keys: bfloat16 [32768, 1024], P(('rep', 'seq')), parts along dimension 0, may hold values from -6 to 6
- cached_values: bfloat16 [32768, 1024], P(('rep', 'seq')), parts along dimension 0, may hold values from -6 to 6
- window_queries: bfloat16 [256, 8192], P(('rep', 'seq')), parts along dimension 0
- kept_count: int32 [32], P(('rep', 'seq')), parts along dimension 0, may hold values from 1 to 640, 8192 in all
- kept_entry: int32 [20480], P(('rep', 'seq')), parts along dimension 0, may hold values from 0 to 8191
- row_owner: int32 [20480], P(('rep', 'seq')), parts along dimension 0, may hold values from 0 to 15, as said below
Outputs:
- importance: float32 [16, 16384], P('rep', 'seq'), parts along dimension 0
- compact_rows: bfloat16 [20480, 256], P(('rep', 'seq')), parts along dimension 0
- compact_score: bfloat16 [20480], P(('rep', 'seq')), parts along dimension 0
There are 2 independent parts, one for each index of `rep`. A program takes and returns all parts, laid end to end along the dimension named above; each array names one. Nothing has to cross between parts.
Inputs may be any that keep to these rules, and one draw needn't show every extreme that they name: `kept_count`: the counts of the 16 devices sum to 8192. `kept_entry`: entries may repeat. `row_owner`: among the 640 slots of one device every owner is named by exactly 40 slots.
All inputs are finite; a program needn't handle non-finite values.
Results may differ from a plain program's by a relative error of at most 0.0004.
Values may be sent and summed in bfloat16 or wider, within the bound.
No kernel may reach another device: no remote copies, remote signals or barrier semaphores. Data moves between devices by JAX's collectives and lax.ppermute only.
A program may use at most 64 MiB of HBM per device.

v0:
```python
import jax
import jax.numpy as jnp
from jax import lax
from jax.sharding import PartitionSpec as P

HEADS = 64
KV_HEADS = 8
HEAD_DIM = 128
GROUP = 8
WINDOW = 128
POOL = 7


def joined(shard, axis, combine):
    everything = jax.tree.map(lambda part: lax.all_gather(part, axis), shard)
    initial = jax.tree.map(lambda part: part[0], everything)

    def lap(k, so_far):
        return combine(so_far, jax.tree.map(lambda part: part[k], everything))

    return lax.fori_loop(1, lax.axis_size(axis), lap, initial)


def with_halo(block, sides, width):
    for axis, dim in sides:
        count = lax.axis_size(axis)
        forward = [(i, i + 1) for i in range(count - 1)]
        backward = [(target, source) for source, target in forward]
        low = lax.ppermute(
            lax.slice_in_dim(block, block.shape[dim] - width, None, axis=dim), axis, forward
        )
        high = lax.ppermute(lax.slice_in_dim(block, 0, width, axis=dim), axis, backward)
        block = jnp.concatenate([low, block, high], axis=dim)
    return block


def grouped(piece):
    row_count = piece.shape[0]
    shaped = piece.reshape(row_count, KV_HEADS, GROUP, HEAD_DIM).transpose(1, 2, 0, 3)
    return shaped.reshape(KV_HEADS, GROUP * row_count, HEAD_DIM)


def group_scores(query_rows, key_rows):
    return jnp.einsum(
        "qd,td->qt", query_rows, key_rows, preferred_element_type=jnp.float32
    ) * HEAD_DIM ** (-0.5)


def by_group(stat, row_count):
    return stat.reshape(KV_HEADS, GROUP * row_count)


def combine_stats(earlier, later):
    highest = jnp.maximum(earlier[0], later[0])
    return (
        highest,
        earlier[1] * jnp.exp(earlier[0] - highest) + later[1] * jnp.exp(later[0] - highest),
    )


def per_device(cached_keys, cached_values, window_queries, kept_count, kept_entry, row_owner):
    positions = cached_keys.shape[0]
    peers = lax.axis_size("seq")
    slots = kept_entry.shape[0]
    capacity = slots // peers
    slot_index = jnp.arange(slots, dtype=jnp.int32)
    is_live = slot_index < kept_count[0]
    member = (
        (row_owner[:, None] == jnp.arange(peers, dtype=jnp.int32)[None, :]) & is_live[:, None]
    ).astype(jnp.int32)
    earlier = jnp.cumsum(member, axis=0) - member
    slot_rank = jnp.sum(earlier * member, axis=1)
    head_index = kept_entry // positions
    token_index = kept_entry % positions
    row_index = token_index * KV_HEADS + head_index
    key_rows = cached_keys.reshape(positions * KV_HEADS, HEAD_DIM)[row_index]
    value_rows = cached_values.reshape(positions * KV_HEADS, HEAD_DIM)[row_index]
    payload = jnp.concatenate([key_rows, value_rows], axis=1)
    target = jnp.where(is_live, row_owner * capacity + slot_rank, peers * capacity)
    send_rows = (
        jnp.zeros((peers * capacity, 2 * HEAD_DIM), jnp.bfloat16)
        .at[target]
        .set(payload, mode="drop")
    )
    send_rows = send_rows.reshape(peers, capacity, 2 * HEAD_DIM)
    key_groups = cached_keys.reshape(positions, KV_HEADS, HEAD_DIM).transpose(1, 0, 2)
    whole = lax.all_gather(window_queries, "seq", axis=0, tiled=True)
    blank = jnp.zeros((HEADS, WINDOW), jnp.float32)

    def run_pass(advance, initial):
        return advance(initial, whole, 0)

    def both_pass(carry, piece, start):
        row_count = piece.shape[0]

        def local_stats(operands):
            scores = group_scores(operands[0], operands[1])
            peak_rows = jnp.max(scores, axis=1)
            return (peak_rows, jnp.sum(jnp.exp(scores - peak_rows[:, None]), axis=1))

        peaks, totals = lax.map(local_stats, (grouped(piece), key_groups))
        new_peak = peaks.reshape(HEADS, row_count)
        new_total = totals.reshape(HEADS, row_count)
        return (new_peak, new_total)

    def mass_pass_for(peak_all, inverse):

        def advance(carry, piece, start):
            row_count = piece.shape[0]
            peaks = by_group(peak_all, row_count)
            weights = by_group(inverse, row_count)

            def local_mass(operands):
                scores = group_scores(operands[0], operands[1])
                return jnp.sum(
                    jnp.exp(scores - operands[2][:, None]) * operands[3][:, None], axis=0
                )

            return carry + lax.map(local_mass, (grouped(piece), key_groups, peaks, weights))

        return advance

    local_peak, local_total = run_pass(both_pass, (blank, blank))
    glob_peak, glob_total = joined((local_peak, local_total), "seq", combine_stats)
    inverse = 1.0 / glob_total
    column_mass = run_pass(
        mass_pass_for(glob_peak, inverse), jnp.zeros((KV_HEADS, positions), jnp.float32)
    )
    padded = with_halo(column_mass, (("seq", 1),), POOL // 2)
    pooled = padded[:, 0:positions]
    for offset in range(1, POOL):
        pooled = pooled + padded[:, offset : offset + positions]
    importance = pooled * (peers * positions / (GROUP * WINDOW * POOL))
    score_rows = importance[head_index, token_index].astype(jnp.bfloat16)
    send_score = (
        jnp.zeros((peers * capacity,), jnp.bfloat16).at[target].set(score_rows, mode="drop")
    )
    send_score = send_score.reshape(peers, capacity)
    got_rows, got_score = (
        lax.all_to_all(send_rows, "seq", split_axis=0, concat_axis=0, tiled=True),
        lax.all_to_all(send_score, "seq", split_axis=0, concat_axis=0, tiled=True),
    )
    return (
        importance,
        got_rows.reshape(peers * capacity, 2 * HEAD_DIM),
        got_score.reshape(peers * capacity),
    )


def solution(mesh):
    in_specs = (
        P(("rep", "seq"), None),
        P(("rep", "seq"), None),
        P(("rep", "seq"), None),
        P(("rep", "seq")),
        P(("rep", "seq")),
        P(("rep", "seq")),
    )
    out_specs = (P("rep", "seq"), P(("rep", "seq"), None), P(("rep", "seq")))
    return jax.shard_map(
        per_device, mesh=mesh, in_specs=in_specs, out_specs=out_specs, check_vma=False
    )
```

profile of v0, /device:TPU:0, one launch (start us, length us, event | category | flops | bytes accessed | tf_op | source)
XLA Modules:
  0.0 182.2 jit_solution(3419498139225878264)
XLA Ops:
  9.3 1.4 reduce-window.6
  11.0 4.3 %reshape.80 = bf16[8192,128]{1,0:T(8,128)(2,1)} reshape(bf16[1024,1024]{1,0:T(8,128)(2,1)} %param.12) | data formatting | bytes 4194304 | tf_op jit(solution)/shard_map/reshape | solution.py:76
  15.3 2.3 %reshape.81 = bf16[8192,128]{1,0:T(8,128)(2,1)} reshape(bf16[1024,1024]{1,0:T(8,128)(2,1)S(1)} %copy-done.2) | data formatting | bytes 4194304 | tf_op jit(solution)/shard_map/reshape | solution.py:77
  17.7 3.7 %gather_fusion = bf16[640,128]{1,0:T(8,128)(2,1)S(1)} fusion(bf16[8192,128]{1,0:T(8,128)(2,1)} %reshape.80, s32[1024]{0:T(1024)S(1)} %pad_clamp_fusion), kind=kCustom, calls=%fused_computation | custom fusion | bytes 330240 | tf_op jit(solution)/shard_map/gather | solution.py:76
  21.4 3.6 %gather_fusion.1 = bf16[640,128]{1,0:T(8,128)(2,1)S(1)} fusion(bf16[8192,128]{1,0:T(8,128)(2,1)} %reshape.81, s32[1024]{0:T(1024)S(1)} %pad_clamp_fusion), kind=kCustom, calls=%fused_computation.1 | custom fusion | bytes 330240 | tf_op jit(solution)/shard_map/gather | solution.py:77
  25.1 6.6 %scatter_custom_fusion = bf16[640,256]{1,0:T(8,128)(2,1)} fusion(s32[640]{0:T(1024)S(1)} %compare_select_fusion.3, bf16[640,128]{1,0:T(8,128)(2,1)S(1)} %gather_fusion.1, bf16[]{:T(256)} %constant.140, bf16[640,128]{1,0:T(8,128)(2,1)S(1)} %gather_fusion, bf16[]{:T(256)} %constant.112.clone.1), kind=kCustom, calls=%fused_computation.26 | custom fusion | flops 655360 | bytes 655364 | tf_op jit(solution)/shard_map/scatter | solution.py:83
  31.7 7.4 %all-to-all-start = ((bf16[16,40,256]{2,1,0:T(8,128)(2,1)}), bf16[16,40,256]{2,1,0:T(8,128)(2,1)S(1)}, u32[]{:S(2)}, u32[]{:S(2)}) async-start(bf16[16,40,256]{2,1,0:T(8,128)(2,1)} %bitcast.22), calls=%async_computation | async-start | bytes 655360 | tf_op jit(solution)/shard_map/all_to_all | solution.py:140
  39.2 2.6 %copy.16 = bf16[1024,1024]{0,1:T(8,128)(2,1)} copy(bf16[1024,1024]{1,0:T(8,128)(2,1)S(1)} %copy-done.1) | data formatting | bytes 4194304 | tf_op args[0]
  41.8 3.0 %copy.18 = bf16[8,1024,128]{2,1,0:T(8,128)(2,1)S(1)} copy(bf16[8,1024,128]{1,2,0:T(8,128)(2,1)} %bitcast.93) | data formatting | bytes 4194304 | tf_op jit(solution)/shard_map/while | solution.py:119
  44.8 12.9 %all-gather.2.cloned.1.call-done = bf16[128,8192]{1,0:T(8,128)(2,1)} async-done(((bf16[8,8192]{1,0:T(8,128)(2,1)}), bf16[128,8192]{1,0:T(8,128)(2,1)}) %all-gather.2.cloned.1.call-update) | async-done | bytes 2097168 | tf_op jit(solution)/shard_map/all_gather | solution.py:87
  57.7 2.2 %copy.22 = bf16[16,8,64,128]{3,2,1,0:T(8,128)(2,1)S(1)} copy(bf16[16,8,64,128]{3,1,2,0:T(8,128)(2,1)} %bitcast.96) | data formatting | bytes 4194304
  59.9 2.7 %copy.15 = bf16[128,8,8,128]{3,0,2,1:T(8,128)(2,1)} copy(bf16[128,8,8,128]{3,2,1,0:T(8,128)(2,1)S(1)} %bitcast.94) | data formatting | bytes 4194304 | tf_op jit(solution)/shard_map/reshape | solution.py:39
  62.6 21.2 %while.39 = (s32[]{:T(128)}, f32[8,1024]{1,0:T(8,128)S(1)}, f32[8,1024]{1,0:T(8,128)S(1)}, bf16[8,1024,128]{2,1,0:T(8,128)(2,1)}, bf16[8,1024,128]{2,1,0:T(8,128)(2,1)S(1)}, /*index=5*/s32[]{:T(128)}, s32[]{:T(128)}) while((s32[]{:T(128)}, f32[8,1024]{1,0:T(8,128)S(1)}, f32[8,1024]{1,0:T(8,128)S(1)}, bf16[8,1024,128]{2,1,0:T(8,128)(2,1)}, ...), condition=%wide.region_3.4_spmd, body=%wide.region_0.3_spmd.sunk | while | flops 273676288 | bytes 8942677 | solution.py:101
  62.6 1.7 multiply_reduce_fusion.4
  64.3 0.7 exponential_reduce_fusion.2
  65.3 1.7 multiply_reduce_fusion.4
  66.9 0.7 exponential_reduce_fusion.2
  67.9 1.7 multiply_reduce_fusion.4
  69.6 0.7 exponential_reduce_fusion.2
  70.6 1.7 multiply_reduce_fusion.4
  72.2 0.7 exponential_reduce_fusion.2
  73.2 1.7 multiply_reduce_fusion.4
  74.9 0.7 exponential_reduce_fusion.2
  75.9 1.7 multiply_reduce_fusion.4
  77.6 0.7 exponential_reduce_fusion.2
  78.5 1.7 multiply_reduce_fusion.4
  80.2 0.7 exponential_reduce_fusion.2
  81.2 1.7 multiply_reduce_fusion.4
  82.9 0.7 exponential_reduce_fusion.2
  83.9 20.8 %all_gather.11 = f32[16,64,128]{2,1,0:T(8,128)S(1)} all-gather(f32[1,64,128]{2,1,0:T(8,128)S(1)} %all_gather_reshape.7), channel_id=1, replica_groups=mesh['rep'=2,'seq'=16] {'seq'}, dimensions={0}, use_global_device_ids=true | all-gather | bytes 557056 | tf_op jit(solution)/shard_map/all_gather | solution.py:15
  104.6 18.9 %all_gather.10 = f32[16,64,128]{2,1,0:T(8,128)S(1)} all-gather(f32[1,64,128]{2,1,0:T(8,128)S(1)} %all_gather_reshape.6), channel_id=1, replica_groups=mesh['rep'=2,'seq'=16] {'seq'}, dimensions={0}, use_global_device_ids=true | all-gather | bytes 557056 | tf_op jit(solution)/shard_map/all_gather | solution.py:15
  123.5 0.8 while.40
  124.4 17.1 %while.41 = (s32[]{:T(128)}, f32[8,1024]{1,0:T(8,128)S(1)}, bf16[8,1024,128]{2,1,0:T(8,128)(2,1)}, bf16[8,1024,128]{2,1,0:T(8,128)(2,1)S(1)}, f32[8,1024]{1,0:T(...) while((s32[]{:T(128)}, f32[8,1024]{1,0:T(8,128)S(1)}, bf16[8,1024,128]{2,1,0:T(8,128)(2,1)}, ...), condition=%wide.region_8.9_spmd, body=%wide.region_6.8_spmd.sunk | while | flops 272628736 | bytes 562269 | solution.py:119
  124.5 2.0 %multiply_reduce_fusion.5 = f32[1024]{0:T(1024)S(1)} fusion(f32[1024]{0:T(1024)S(1)} %bitcast.101, f32[1024]{0:T(1024)S(1)} %bitcast.102, bf16[8,1024,128]{2,1,0:T(8,128)(2,1)S(1)} %get-tuple-element.440, s32[]{:T(128)} %get-tuple-element.429, bf16[8,1024,128]{2,1,0:T(8,128)(2,1)} %get-tuple-element.439), kind=kOutput, calls=%fused_computation.18.clone.1 | convolution fusion | flops 272628736 | bytes 537600 | tf_op jit(solution)/shard_map/while/body/eval_jaxpr/qd,td->qt/dot_general | solution.py:44
  126.6 2.0 %multiply_reduce_fusion.5 = f32[1024]{0:T(1024)S(1)} fusion(f32[1024]{0:T(1024)S(1)} %bitcast.101, f32[1024]{0:T(1024)S(1)} %bitcast.102, bf16[8,1024,128]{2,1,0:T(8,128)(2,1)S(1)} %get-tuple-element.440, s32[]{:T(128)} %get-tuple-element.429, bf16[8,1024,128]{2,1,0:T(8,128)(2,1)} %get-tuple-element.439), kind=kOutput, calls=%fused_computation.18.clone.1 | convolution fusion | flops 272628736 | bytes 537600 | tf_op jit(solution)/shard_map/while/body/eval_jaxpr/qd,td->qt/dot_general | solution.py:44
  128.7 2.0 %multiply_reduce_fusion.5 = f32[1024]{0:T(1024)S(1)} fusion(f32[1024]{0:T(1024)S(1)} %bitcast.101, f32[1024]{0:T(1024)S(1)} %bitcast.102, bf16[8,1024,128]{2,1,0:T(8,128)(2,1)S(1)} %get-tuple-element.440, s32[]{:T(128)} %get-tuple-element.429, bf16[8,1024,128]{2,1,0:T(8,128)(2,1)} %get-tuple-element.439), kind=kOutput, calls=%fused_computation.18.clone.1 | convolution fusion | flops 272628736 | bytes 537600 | tf_op jit(solution)/shard_map/while/body/eval_jaxpr/qd,td->qt/dot_general | solution.py:44
  130.9 2.0 %multiply_reduce_fusion.5 = f32[1024]{0:T(1024)S(1)} fusion(f32[1024]{0:T(1024)S(1)} %bitcast.101, f32[1024]{0:T(1024)S(1)} %bitcast.102, bf16[8,1024,128]{2,1,0:T(8,128)(2,1)S(1)} %get-tuple-element.440, s32[]{:T(128)} %get-tuple-element.429, bf16[8,1024,128]{2,1,0:T(8,128)(2,1)} %get-tuple-element.439), kind=kOutput, calls=%fused_computation.18.clone.1 | convolution fusion | flops 272628736 | bytes 537600 | tf_op jit(solution)/shard_map/while/body/eval_jaxpr/qd,td->qt/dot_general | solution.py:44
  133.0 2.0 %multiply_reduce_fusion.5 = f32[1024]{0:T(1024)S(1)} fusion(f32[1024]{0:T(1024)S(1)} %bitcast.101, f32[1024]{0:T(1024)S(1)} %bitcast.102, bf16[8,1024,128]{2,1,0:T(8,128)(2,1)S(1)} %get-tuple-element.440, s32[]{:T(128)} %get-tuple-element.429, bf16[8,1024,128]{2,1,0:T(8,128)(2,1)} %get-tuple-element.439), kind=kOutput, calls=%fused_computation.18.clone.1 | convolution fusion | flops 272628736 | bytes 537600 | tf_op jit(solution)/shard_map/while/body/eval_jaxpr/qd,td->qt/dot_general | solution.py:44
  135.1 2.0 %multiply_reduce_fusion.5 = f32[1024]{0:T(1024)S(1)} fusion(f32[1024]{0:T(1024)S(1)} %bitcast.101, f32[1024]{0:T(1024)S(1)} %bitcast.102, bf16[8,1024,128]{2,1,0:T(8,128)(2,1)S(1)} %get-tuple-element.440, s32[]{:T(128)} %get-tuple-element.429, bf16[8,1024,128]{2,1,0:T(8,128)(2,1)} %get-tuple-element.439), kind=kOutput, calls=%fused_computation.18.clone.1 | convolution fusion | flops 272628736 | bytes 537600 | tf_op jit(solution)/shard_map/while/body/eval_jaxpr/qd,td->qt/dot_general | solution.py:44
  137.3 2.0 %multiply_reduce_fusion.5 = f32[1024]{0:T(1024)S(1)} fusion(f32[1024]{0:T(1024)S(1)} %bitcast.101, f32[1024]{0:T(1024)S(1)} %bitcast.102, bf16[8,1024,128]{2,1,0:T(8,128)(2,1)S(1)} %get-tuple-element.440, s32[]{:T(128)} %get-tuple-element.429, bf16[8,1024,128]{2,1,0:T(8,128)(2,1)} %get-tuple-element.439), kind=kOutput, calls=%fused_computation.18.clone.1 | convolution fusion | flops 272628736 | bytes 537600 | tf_op jit(solution)/shard_map/while/body/eval_jaxpr/qd,td->qt/dot_general | solution.py:44
  139.4 2.0 %multiply_reduce_fusion.5 = f32[1024]{0:T(1024)S(1)} fusion(f32[1024]{0:T(1024)S(1)} %bitcast.101, f32[1024]{0:T(1024)S(1)} %bitcast.102, bf16[8,1024,128]{2,1,0:T(8,128)(2,1)S(1)} %get-tuple-element.440, s32[]{:T(128)} %get-tuple-element.429, bf16[8,1024,128]{2,1,0:T(8,128)(2,1)} %get-tuple-element.439), kind=kOutput, calls=%fused_computation.18.clone.1 | convolution fusion | flops 272628736 | bytes 537600 | tf_op jit(solution)/shard_map/while/body/eval_jaxpr/qd,td->qt/dot_general | solution.py:44
  141.6 1.3 collective-permute-start.1
  142.9 3.2 %collective-permute-start = (f32[8,3]{1,0:T(8,128)S(1)}, f32[8,3]{1,0:T(8,128)S(1)}, u32[]{:S(2)}, u32[]{:S(2)}) collective-permute-start(f32[8,3]{1,0:T(8,128)S(1)} %get-tuple-element.262), channel_id=1, source_target_pairs={{0,1},{1,2},{2,3},{3,4},{4,5},{5,6},{6,7},{7,8},{8,9},{9,10},{10,1... | collective-permute-start | bytes 296 | tf_op jit(solution)/shard_map/ppermute | solution.py:29
  146.9 4.2 %gather_fusion.2 = bf16[640]{0:T(1024)(128)(2,1)S(1)} fusion(f32[8,1024]{1,0:T(8,128)S(1)} %fusion.31, s32[640]{0:T(1024)S(1)} %get-tuple-element.263), kind=kCustom, calls=%fused_computation.2 | custom fusion | bytes 7680 | tf_op jit(solution)/shard_map/gather | solution.py:134
  151.0 8.6 %scatter_custom_fusion.1 = bf16[640]{0:T(1024)(128)(2,1)S(1)} fusion(s32[640]{0:T(1024)S(1)} %compare_select_fusion.3, bf16[640]{0:T(1024)(128)(2,1)S(1)} %gather_fusion.2, bf16[]{:T(256)} %constant.112.clone.1), kind=kCustom, calls=%fused_computation.81 | custom fusion | bytes 1282 | tf_op jit(solution)/shard_map/scatter | solution.py:136
  160.4 7.1 %all-to-all-start.1 = ((bf16[16,1,40]{2,1,0:T(2,128)(2,1)}), bf16[16,1,40]{2,1,0:T(2,128)(2,1)S(1)}, u32[]{:S(2)}, u32[]{:S(2)}) async-start(bf16[16,1,40]{2,1,0:T(2,128)(2,1)} %all_to_all.12), calls=%async_computation.1 | async-start | bytes 16384 | tf_op jit(solution)/shard_map/all_to_all | solution.py:141
  167.5 6.4 %all-to-all-done.1 = bf16[16,1,40]{2,1,0:T(2,128)(2,1)S(1)} async-done(((bf16[16,1,40]{2,1,0:T(2,128)(2,1)}), bf16[16,1,40]{2,1,0:T(2,128)(2,1)S(1)}, u32[]{:S(2)}, u32[]{:S(2)}) %all-to-all-start.1) | async-done | bytes 1312 | tf_op jit(solution)/shard_map/all_to_all | solution.py:141
  174.6 0.7 copy.54
  (88 shorter events, 7.2 us)
Async XLA Ops:
  7.2 50.5 %all-gather.2.cloned.1.call-start = ((), (), s32[]{:S(2)}) async-start(), calls=%async_computation.2 | async-start | bytes 2228224 | tf_op jit(solution)/shard_map/all_gather | solution.py:87
  11.0 4.3 %copy-start.2 = (bf16[1024,1024]{1,0:T(8,128)(2,1)S(1)}, bf16[1024,1024]{1,0:T(8,128)(2,1)}, u32[]{:S(2)}) copy-start(bf16[1024,1024]{1,0:T(8,128)(2,1)} %param.13) | copy-start | bytes 6291460
  15.3 2.3 %copy-start.4 = (s32[640]{0:T(1024)S(1)}, s32[640]{0:T(1024)}, u32[]{:S(2)}) copy-start(s32[640]{0:T(1024)} %param.16) | copy-start | bytes 7684
  17.6 7.4 %copy-start.3 = (s32[640]{0:T(1024)S(1)}, s32[640]{0:T(1024)}, u32[]{:S(2)}) copy-start(s32[640]{0:T(1024)} %param.17) | copy-start | bytes 7684
  17.6 21.5 %copy-start.1 = (bf16[1024,1024]{1,0:T(8,128)(2,1)S(1)}, bf16[1024,1024]{1,0:T(8,128)(2,1)}, u32[]{:S(2)}) copy-start(bf16[1024,1024]{1,0:T(8,128)(2,1)} %param.12) | copy-start | bytes 6291460
  31.7 128.6 %all-to-all-start = ((bf16[16,40,256]{2,1,0:T(8,128)(2,1)}), bf16[16,40,256]{2,1,0:T(8,128)(2,1)S(1)}, u32[]{:S(2)}, u32[]{:S(2)}) async-start(bf16[16,40,256]{2,1,0:T(8,128)(2,1)} %bitcast.22), calls=%async_computation | async-start | bytes 655360 | tf_op jit(solution)/shard_map/all_to_all | solution.py:140
  141.6 4.5 %collective-permute-start.1 = (f32[8,3]{1,0:T(8,128)S(1)}, f32[8,3]{1,0:T(8,128)S(1)}, u32[]{:S(2)}, u32[]{:S(2)}) collective-permute-start(f32[8,3]{1,0:T(8,128)S(1)} %get-tuple-element.261), channel_id=1, source_target_pairs={{1,0},{2,1},{3,2},{4,3},{5,4},{6,5},{7,6},{8,7},{9,8},{10,9},{11,1... | collective-permute-start | bytes 296 | tf_op jit(solution)/shard_map/ppermute | solution.py:32
  142.9 3.8 %collective-permute-start = (f32[8,3]{1,0:T(8,128)S(1)}, f32[8,3]{1,0:T(8,128)S(1)}, u32[]{:S(2)}, u32[]{:S(2)}) collective-permute-start(f32[8,3]{1,0:T(8,128)S(1)} %get-tuple-element.262), channel_id=1, source_target_pairs={{0,1},{1,2},{2,3},{3,4},{4,5},{5,6},{6,7},{7,8},{8,9},{9,10},{10,1... | collective-permute-start | bytes 296 | tf_op jit(solution)/shard_map/ppermute | solution.py:29
  146.8 28.5 %copy-start = (f32[8,1024]{1,0:T(8,128)}, f32[8,1024]{1,0:T(8,128)S(1)}, u32[]{:S(2)}) copy-start(f32[8,1024]{1,0:T(8,128)S(1)} %fusion.31) | copy-start | bytes 98308
  160.4 13.5 %all-to-all-start.1 = ((bf16[16,1,40]{2,1,0:T(2,128)(2,1)}), bf16[16,1,40]{2,1,0:T(2,128)(2,1)S(1)}, u32[]{:S(2)}, u32[]{:S(2)}) async-start(bf16[16,1,40]{2,1,0:T(2,128)(2,1)} %all_to_all.12), calls=%async_computation.1 | async-start | bytes 16384 | tf_op jit(solution)/shard_map/all_to_all | solution.py:141
Sparse Core Ops, SparseCore 0:
  10.2 47.4 all-gather.1
where the time goes:
time: 183 us; the launch traced here: 182 us
  local copies, waits for them, and re-layouts  42.4 us (23%)
  blocking collectives  39.6 us (22%)
  matrix products  29.2 us (16%)
  waiting for transfers between devices  20.6 us (11%)
  starting transfers between devices  19.1 us (10%)
  other arithmetic  15.4 us (8%)
  between operations  14.9 us (8%)
    all_gather x2, blocking collectives, joined(): everything = jax.tree.map(lambda part: lax.all_gather(part, axis), shard)  39.6 us
    dot_general x16, matrix products, group_scores(): jnp.einsum('qd,td->qt', query_rows, key_rows, preferred_element_type=jnp....  29.2 us
    all_gather x1, waiting for transfers between devices, per_device(): whole = lax.all_gather(window_queries, 'seq', axis=0, tiled=True)  12.9 us
    scatter x1, local copies, waits for them, and re-layouts, per_device(): jnp.zeros((peers * capacity,), jnp.bfloat16).at[target]  8.61 us
    all_to_all x1, starting transfers between devices, per_device(): lax.all_to_all(send_rows, 'seq', split_axis=0, concat_axis=0, tiled=True)  7.44 us
    all_to_all x1, starting transfers between devices, per_device(): lax.all_to_all(send_score, 'seq', split_axis=0, concat_axis=0, tiled=True)  7.09 us
    scatter x1, other arithmetic, per_device(): send_rows = jnp.zeros((peers * capacity, 2 * HEAD_DIM), jnp.bfloat16).at[...  6.64 us
    all_to_all x1, waiting for transfers between devices, per_device(): lax.all_to_all(send_score, 'seq', split_axis=0, concat_axis=0, tiled=True)  6.41 us
  transfers between devices with their start and end apart: 5, of which 3 were waited for; matrix products, arithmetic and copies ran while one was open for 47% of the time, Pallas kernels for 0%

commit v1 on v0

v1 whole, which is shorter than its diff:
```python
import functools

import jax
import jax.numpy as jnp
from jax import lax
from jax.experimental import pallas as pl
from jax.experimental.pallas import tpu as pltpu
from jax.sharding import PartitionSpec as P

HEADS = 64
KV_HEADS = 8
HEAD_DIM = 128
GROUP = 8
WINDOW = 128
POOL = 7
HALF = KV_HEADS // 2
EDGE = 16
SCALE2 = HEAD_DIM ** (-0.5) * 1.4426950408889634
MIB = 1 << 20

VMEM = pl.BlockSpec(memory_space=pltpu.VMEM)
SMEM = pl.BlockSpec(memory_space=pltpu.SMEM)


def nt(a, b, precision=None):
    return lax.dot_general(
        a, b, (((1,), (1,)), ((), ())), precision=precision, preferred_element_type=jnp.float32
    )


def one_hot(mask):
    return jnp.where(mask, 1.0, 0.0).astype(jnp.bfloat16)


def iota(shape, dim):
    return lax.broadcasted_iota(jnp.int32, shape, dim)


def compact_kernel(peers, count_ref, entry_ref, owner_ref, k_ref, v_ref, rows_ref, code_ref):
    positions = k_ref.shape[0]
    slots = entry_ref.shape[1]
    capacity = slots // peers
    owner, entry = owner_ref[...], entry_ref[...]
    live = iota((1, slots), 1) < count_ref[0]
    member = jnp.where((owner == iota((peers, slots), 0)) & live, 1.0, 0.0)
    before = one_hot(iota((slots, slots), 0) < iota((slots, slots), 1))
    earlier = jnp.dot(member.astype(jnp.bfloat16), before, preferred_element_type=jnp.float32)
    rank = jnp.sum(earlier * member, axis=0, keepdims=True).astype(jnp.int32)
    target = jnp.where(live, owner * capacity + rank, -1)
    placed = one_hot(iota((slots, slots), 0) == target)
    token, head = entry % positions, entry // positions
    line = iota((8, slots), 0)
    facts = jnp.where(
        line == 0, 1, jnp.where(line == 1, head, jnp.where(line == 2, token // 64, token % 64))
    )
    facts = facts.astype(jnp.float32).astype(jnp.bfloat16)
    by_row = nt(facts, placed)
    row_token = jnp.where(by_row[0:1] > 0.5, by_row[2:3] * 64 + by_row[3:4], -1.0)
    code_ref[...] = jnp.where(iota((8, slots), 0) == 0, row_token, by_row[1:2])
    by_col = nt(placed, facts)
    col_head = by_col[:, 1:2].astype(jnp.int32)
    col_token = jnp.where(by_col[:, 0:1] > 0.5, by_col[:, 2:3] * 64 + by_col[:, 3:4], -1.0)
    col_token = col_token.astype(jnp.int32)
    step = 128 if slots % 128 == 0 else slots
    for start in range(0, slots, step):
        token_part = col_token[start : start + step]
        head_part = col_head[start : start + step]
        pick = one_hot(iota((step, positions), 1) == token_part)
        for side, source in enumerate((k_ref, v_ref)):
            found = jnp.dot(pick, source[...], preferred_element_type=jnp.float32)
            kept = jnp.zeros((step, HEAD_DIM), jnp.float32)
            for g in range(KV_HEADS):
                part = found[:, g * HEAD_DIM : (g + 1) * HEAD_DIM]
                kept = kept + jnp.where(head_part == g, part, 0.0)
            rows_ref[start : start + step, side * HEAD_DIM : (side + 1) * HEAD_DIM] = kept.astype(
                jnp.bfloat16
            )


def query_rows(block_refs, g):
    parts = []
    for ref in block_refs:
        for h in range(GROUP):
            first = (g * GROUP + h) * HEAD_DIM
            parts.append(ref[:, first : first + HEAD_DIM])
    return jnp.concatenate(parts, axis=0)


def local_stats(block_refs, k_refs, store):
    per_block = GROUP * block_refs[0].shape[0]
    for g in range(HALF):
        rows = query_rows(block_refs, g)
        count = rows.shape[0]
        peak = jnp.full((1, count), -jnp.inf, jnp.float32)
        total = jnp.zeros((1, count), jnp.float32)
        for k_ref in k_refs:
            tokens = k_ref.shape[0]
            step = min(512, tokens)
            for start in range(0, tokens, step):
                keys = k_ref[start : start + step, g * HEAD_DIM : (g + 1) * HEAD_DIM]
                scores = nt(keys, rows)
                higher = jnp.maximum(peak, jnp.max(scores, axis=0, keepdims=True))
                total = total * jnp.exp2((peak - higher) * SCALE2) + jnp.sum(
                    jnp.exp2((scores - higher) * SCALE2), axis=0, keepdims=True
                )
                peak = higher
        lse = peak * SCALE2 + jnp.log2(total)
        for b in range(len(block_refs)):
            store(b, g, lse[:, b * per_block : (b + 1) * per_block])


def sender(chip, offset):
    return 0 if offset is None else chip ^ offset


def early_stats_kernel(count, *refs):
    blocks, (k_own, k_sib), out_ref = refs[:count], refs[count : count + 2], refs[-1]

    def store(b, g, lse):
        out_ref[b, g : g + 1, :] = lse

    local_stats(blocks, (k_own, k_sib), store)


def stats_kernel(offsets, early, dests, *refs):
    place_ref, refs = refs[0], refs[1:]
    if early:
        early_ref, refs = refs[0], refs[1:]
    late = len(offsets) - early
    blocks, (k_own, k_sib), out_ref, hold = (
        refs[:late], refs[late : late + 2], refs[late + 2], refs[late + 3])
    chip = place_ref[0] // 2

    for b in range(early):
        hold[sender(chip, offsets[b])] = early_ref[b]

    def store(b, g, lse):
        hold[sender(chip, offsets[early + b]), g : g + 1, :] = lse

    local_stats(blocks, (k_own, k_sib), store)
    everything = hold[...]
    for d in range(dests):
        out_ref[d] = everything


def split3(x):
    high = x.astype(jnp.bfloat16)
    rest = x - high.astype(jnp.float32)
    middle = rest.astype(jnp.bfloat16)
    low = (rest - middle.astype(jnp.float32)).astype(jnp.bfloat16)
    return high, middle, low


def mass_kernel(offsets, peers, factor, *refs):
    place_ref, stats_ref, code_own_ref, code_sib_ref = refs[:4]
    blocks = refs[4 : 4 + len(offsets)]
    k_own, k_sib, edge_own, edge_sib, imp_own, imp_sib, score_ref, lse_ref = refs[4 + len(offsets) :]
    tokens = k_own.shape[0]
    core = place_ref[0] % 2
    chip = place_ref[0] // 2
    chips = peers // 2
    is_low = core == 0

    stats = stats_ref[...]
    top = jnp.max(stats, axis=0)
    lse_ref[...] = top + jnp.log2(jnp.sum(jnp.exp2(stats - top[None]), axis=0))

    ones = jnp.ones((8, HEAD_DIM), jnp.float32)
    masses = []
    for which, (k_ref, first_col) in enumerate(
        ((k_own, None), (k_sib, None), (edge_own, core), (edge_sib, core))
    ):
        found = []
        for g in range(HALF):
            rows = query_rows(blocks, g)
            lse = jnp.concatenate(
                [lse_ref[sender(chip, off), g : g + 1, :] for off in offsets], axis=1
            )
            step = min(512, k_ref.shape[0])
            for start in range(0, k_ref.shape[0], step):
                cols = slice(g * HEAD_DIM, (g + 1) * HEAD_DIM)
                if first_col is None:
                    keys = k_ref[start : start + step, cols]
                else:
                    low = k_ref[start : start + step, cols]
                    high = k_ref[
                        start : start + step,
                        (HALF + g) * HEAD_DIM : (HALF + g + 1) * HEAD_DIM,
                    ]
                    keys = jnp.where(is_low, low, high)
                weights = jnp.exp2(nt(keys, rows) * SCALE2 - lse)
                folded = weights[:, 0:HEAD_DIM]
                for first in range(HEAD_DIM, weights.shape[1], HEAD_DIM):
                    folded = folded + weights[:, first : first + HEAD_DIM]
                found.append(nt(ones, folded, lax.Precision.HIGHEST)[0:1])
        per_head = len(found) // HALF
        masses.append(
            jnp.concatenate(
                [jnp.concatenate(found[g * per_head : (g + 1) * per_head], axis=1) for g in range(HALF)],
                axis=0,
            )
        )
    own, sib, rim_own, rim_sib = masses
    first = jnp.where(is_low, own, sib)
    second = jnp.where(is_low, sib, own)
    before = jnp.where(is_low, rim_own, rim_sib)[:, EDGE - POOL // 2 :]
    after = jnp.where(is_low, rim_sib, rim_own)[:, : POOL // 2]
    before = jnp.where(chip == 0, 0.0, before)
    after = jnp.where(chip == chips - 1, 0.0, after)
    padded = jnp.concatenate([before, first, second, after], axis=1)
    pooled = padded[:, 0 : 2 * tokens]
    for shift in range(1, POOL):
        pooled = pooled + padded[:, shift : shift + 2 * tokens]
    importance = pooled * factor
    halves = (importance[:, :tokens], importance[:, tokens:])
    imp_own[...] = jnp.where(is_low, halves[0], halves[1])
    imp_sib[...] = jnp.where(is_low, halves[1], halves[0])
    slots = code_own_ref.shape[1]
    capacity = slots // peers
    for side in range(2):
        code = jnp.where(core == side, code_own_ref[...], code_sib_ref[...]).astype(jnp.int32)
        parts = jnp.concatenate(split3(halves[side]), axis=0)
        pick = one_hot(iota((tokens, slots), 0) == code[0:1])
        hits = jnp.dot(parts, pick, preferred_element_type=jnp.float32)
        value = hits[0:HALF] + hits[HALF : 2 * HALF] + hits[2 * HALF : 3 * HALF]
        mine = iota((HALF, slots), 0) + core * HALF == code[1:2]
        score = jnp.sum(jnp.where(mine, value, 0.0), axis=0, keepdims=True)
        for p in range(peers):
            score_ref[p, side : side + 1, 0:capacity] = score[:, p * capacity : (p + 1) * capacity]


def per_device(cached_keys, cached_values, window_queries, kept_count, kept_entry, row_owner):
    positions = cached_keys.shape[0]
    peers = lax.axis_size("seq")
    chips = peers // 2
    slots = kept_entry.shape[0]
    capacity = slots // peers
    me = lax.axis_index("seq")
    core = me % 2
    place = me.astype(jnp.int32).reshape(1)
    half_keys = HALF * HEAD_DIM
    half_queries = HALF * GROUP * HEAD_DIM

    def swap(x, distance):
        return lax.ppermute(x, "seq", [(i, i ^ distance) for i in range(peers)])

    def half(x, which, width):
        return lax.dynamic_slice_in_dim(x, which * width, width, axis=1)

    sibling_queries = swap(window_queries, 1)
    piece = jnp.concatenate(
        [half(window_queries, core, half_queries), half(sibling_queries, core, half_queries)], axis=0
    )
    lines = chips // 2
    if piece.shape[0] % 16 == 0 and chips % 2 == 0 and lines & (lines - 1) == 0:
        far = [swap(piece, 4 * d) for d in range(1, lines)]
        near = [piece, swap(piece, 2)]
        across = swap(jnp.concatenate(far, axis=0), 2)
        rows = piece.shape[0]
        blocks = near + far + [across[i * rows : (i + 1) * rows] for i in range(lines - 1)]
        offsets = [0, 1] + [2 * d for d in range(1, lines)] + [2 * d + 1 for d in range(1, lines)]
        early = 1 + lines
    else:
        same_core = [[i for i in range(peers) if i % 2 == c] for c in range(2)]
        blocks = [lax.all_gather(piece, "seq", axis=0, tiled=True, axis_index_groups=same_core)]
        offsets, early = [None], 0
    count = len(blocks)

    k_own = half(cached_keys, core, half_keys)
    k_sib = swap(half(cached_keys, 1 - core, half_keys), 1)
    rim = jnp.where(core == 1, cached_keys[positions - EDGE :], cached_keys[:EDGE])
    ring = [(2 * i + 1, 2 * i + 2) for i in range(chips - 1)]
    edge_own = lax.ppermute(rim, "seq", ring + [(b, a) for a, b in ring])
    edge_sib = swap(edge_own, 1)

    rows_out, code_own = pl.pallas_call(
        functools.partial(compact_kernel, peers),
        out_shape=(
            jax.ShapeDtypeStruct((slots, 2 * HEAD_DIM), jnp.bfloat16),
            jax.ShapeDtypeStruct((8, slots), jnp.float32),
        ),
        in_specs=[SMEM, VMEM, VMEM, VMEM, VMEM],
        out_specs=(VMEM, VMEM),
        compiler_params=pltpu.CompilerParams(vmem_limit_bytes=32 * MIB),
        name="compact",
    )(kept_count, kept_entry.reshape(1, slots), row_owner.reshape(1, slots), cached_keys, cached_values)
    code_sib = swap(code_own, 1)
    got_rows = lax.all_to_all(
        rows_out.reshape(peers, capacity, 2 * HEAD_DIM), "seq", split_axis=0, concat_axis=0, tiled=True
    )

    per_block = GROUP * blocks[0].shape[0]
    first = []
    if early:
        first = [
            pl.pallas_call(
                functools.partial(early_stats_kernel, early),
                out_shape=jax.ShapeDtypeStruct((early, HALF, per_block), jnp.float32),
                in_specs=[VMEM] * (early + 2),
                out_specs=VMEM,
                compiler_params=pltpu.CompilerParams(vmem_limit_bytes=32 * MIB),
                name="early_stats",
            )(*blocks[:early], k_own, k_sib)
        ]
    sent = pl.pallas_call(
        functools.partial(stats_kernel, offsets, early, chips),
        out_shape=jax.ShapeDtypeStruct((chips, count, HALF, per_block), jnp.float32),
        in_specs=[SMEM] + [VMEM] * (len(first) + count - early + 2),
        out_specs=VMEM,
        scratch_shapes=[pltpu.VMEM((count, HALF, per_block), jnp.float32)],
        compiler_params=pltpu.CompilerParams(vmem_limit_bytes=32 * MIB),
        name="late_stats",
    )(place, *first, *blocks[early:], k_own, k_sib)
    stats = lax.all_to_all(
        sent,
        "seq",
        split_axis=0,
        concat_axis=0,
        tiled=True,
        axis_index_groups=[[i for i in range(peers) if i % 2 == c] for c in range(2)],
    )

    factor = peers * positions / (GROUP * WINDOW * POOL)
    imp_own, imp_sib, score = pl.pallas_call(
        functools.partial(mass_kernel, offsets, peers, factor),
        out_shape=(
            jax.ShapeDtypeStruct((HALF, positions), jnp.float32),
            jax.ShapeDtypeStruct((HALF, positions), jnp.float32),
            jax.ShapeDtypeStruct((peers, 2, 128), jnp.float32),
        ),
        in_specs=[SMEM] + [VMEM] * (7 + count),
        out_specs=(VMEM, VMEM, VMEM),
        scratch_shapes=[pltpu.VMEM((count, HALF, per_block), jnp.float32)],
        compiler_params=pltpu.CompilerParams(vmem_limit_bytes=48 * MIB),
        name="mass",
    )(place, stats, code_own, code_sib, *blocks, k_own, k_sib, edge_own, edge_sib)

    got_score = lax.all_to_all(score, "seq", split_axis=0, concat_axis=0, tiled=True)
    by_core = got_score.reshape(chips, 2, 2, 128)[..., :capacity]
    score_out = (by_core[:, 0] + by_core[:, 1]).astype(jnp.bfloat16)
    imp_other = swap(imp_sib, 1)
    importance = jnp.where(
        core == 0,
        jnp.concatenate([imp_own, imp_other], axis=0),
        jnp.concatenate([imp_other, imp_own], axis=0),
    )
    return (
        importance,
        got_rows.reshape(peers * capacity, 2 * HEAD_DIM),
        score_out.reshape(peers * capacity),
    )


def solution(mesh):
    in_specs = (
        P(("rep", "seq"), None),
        P(("rep", "seq"), None),
        P(("rep", "seq"), None),
        P(("rep", "seq")),
        P(("rep", "seq")),
        P(("rep", "seq")),
    )
    out_specs = (P("rep", "seq"), P(("rep", "seq"), None), P(("rep", "seq")))
    return jax.shard_map(
        per_device, mesh=mesh, in_specs=in_specs, out_specs=out_specs, check_vma=False
    )
```

time: 183 us -> 99.3 us (0.54)
  blocking collectives: 39.6 us -> 0 us
  local copies, waits for them, and re-layouts: 42.4 us -> 8.86 us
  matrix products: 29.2 us -> 0 us
  Pallas kernels: 0 us -> 26.3 us
  starting transfers between devices: 19.1 us -> 34.9 us
  other arithmetic: 15.4 us -> 1.46 us
  between operations: 14.9 us -> 1.43 us
  waiting for transfers between devices: 20.6 us -> 25.7 us
    all_gather x2 -> x0, blocking collectives: 39.6 us -> none  [joined(): everything = jax.tree.map(lambda part: lax.all_gather(part, axis), shard)]
    dot_general x16 -> x0, matrix products: 29.2 us -> none  [group_scores(): jnp.einsum('qd,td->qt', query_rows, key_rows, preferred_element_type=jnp....]
    pallas_call x0 -> x4, Pallas kernels: none -> 26.3 us  [the longest x1 13.2 us: per_device(): pl.pallas_call(functools.partial(mass_kernel, offsets, peers, factor), ou...]
    ppermute x2 -> x11, waiting for transfers between devices: 0.61 us -> 19.9 us  [the longest x10 19.9 us: swap(): return lax.ppermute(x, 'seq', [(i, i ^ distance) for i in range(peers)])]
    all_gather x1 -> x0, waiting for transfers between devices: 12.9 us -> none  [per_device(): whole = lax.all_gather(window_queries, 'seq', axis=0, tiled=True)]
    gather x3 -> x0, local copies, waits for them, and re-layouts: 11.5 us -> none  [the longest x1 4.19 us: per_device(): score_rows = importance[head_index, token_index].astype(jnp.bfloat16)]
    ppermute x2 -> x11, starting transfers between devices: 4.49 us -> 14.7 us  [the longest x10 14 us: swap(): return lax.ppermute(x, 'seq', [(i, i ^ distance) for i in range(peers)])]
    reshape x6 -> x2, local copies, waits for them, and re-layouts: 10 us -> 0.01 us  [the longest x1 0.01 us: per_device(): kept_entry.reshape(1, slots)]
  transfers between devices with their start and end apart: 5 -> 14, of which waited for: 3 -> 7; matrix products, arithmetic and copies ran while one was open for 47% -> 4% of each run, Pallas kernels for 0% -> 18%
where the time goes in v1:
time: 99.3 us; the launch traced here: 98.7 us
  starting transfers between devices  34.9 us (35%)
  Pallas kernels  26.3 us (26%)
  waiting for transfers between devices  25.7 us (26%)
  local copies, waits for them, and re-layouts  8.86 us (9%)
  other arithmetic  1.46 us (1%)
  between operations  1.43 us (1%)
    ppermute x10, waiting for transfers between devices, swap(): return lax.ppermute(x, 'seq', [(i, i ^ distance) for i in range(peers)])  19.9 us
    ppermute x10, starting transfers between devices, swap(): return lax.ppermute(x, 'seq', [(i, i ^ distance) for i in range(peers)])  14 us
    pallas_call x1, Pallas kernels, per_device(): pl.pallas_call(functools.partial(mass_kernel, offsets, peers, factor), ou...  13.2 us
    all_to_all x1, starting transfers between devices, per_device(): lax.all_to_all(score, 'seq', split_axis=0, concat_axis=0, tiled=True)  7.57 us
    all_to_all x1, starting transfers between devices, per_device(): lax.all_to_all(sent, 'seq', split_axis=0, concat_axis=0, tiled=True, axis...  6.54 us
    all_to_all x1, starting transfers between devices, per_device(): lax.all_to_all(rows_out.reshape(peers, capacity, 2 * HEAD_DIM), 'seq', sp...  6.14 us
    all_to_all x1, waiting for transfers between devices, per_device(): lax.all_to_all(score, 'seq', split_axis=0, concat_axis=0, tiled=True)  5.85 us
    unnamed x11, local copies, waits for them, and re-layouts  5.62 us
  transfers between devices with their start and end apart: 14, of which 7 were waited for; matrix products, arithmetic and copies ran while one was open for 4% of the time, Pallas kernels for 18%

profile of v1, /device:TPU:0, one launch (start us, length us, event | category | flops | bytes accessed | tf_op | source)
XLA Modules:
  0.0 98.7 jit_solution(3460059398419631564)
XLA Ops:
  0.6 0.5 collective-permute-start
  1.1 0.8 constant_dynamic-slice_fusion.3
  2.0 0.4 collective-permute-done
  2.4 3.0 %collective-permute-start.2 = (bf16[16,4096]{1,0:T(8,128)(2,1)S(1)}, bf16[16,4096]{1,0:T(8,128)(2,1)S(1)}, u32[]{:S(2)}, u32[]{:S(2)}) collective-permute-start(bf16[16,4096]{1,0:T(8,128)(2,1)S(1)} %pad_maximum_fusion.1.refs_0_.refs_4_), channel_id=1, source_target_pairs={{0,4},{1,5},{2,6},{3,7},{4,0},{5,1},{6,2},{7,3},{8,12},{9,13},{10,... | collective-permute-start | bytes 393224 | tf_op jit(solution)/shard_map/ppermute | solution.py:245
  5.4 2.6 %collective-permute-start.3 = (bf16[16,4096]{1,0:T(8,128)(2,1)S(1)}, bf16[16,4096]{1,0:T(8,128)(2,1)S(1)}, u32[]{:S(2)}, u32[]{:S(2)}) collective-permute-start(bf16[16,4096]{1,0:T(8,128)(2,1)S(1)} %pad_maximum_fusion.1.refs_0_.refs_4_), channel_id=1, source_target_pairs={{0,8},{1,9},{2,10},{3,11},{4,12},{5,13},{6,14},{7,15},{8,0},{9,1},... | collective-permute-start | bytes 393224 | tf_op jit(solution)/shard_map/ppermute | solution.py:245
  8.0 0.0 collective-permute-start.4
  8.0 3.1 %collective-permute-done.2.refs_2_.refs_6_ = bf16[16,4096]{1,0:T(8,128)(2,1)S(1)} collective-permute-done((bf16[16,4096]{1,0:T(8,128)(2,1)S(1)}, bf16[16,4096]{1,0:T(8,128)(2,1)S(1)}, u32[]{:S(2)}, u32[]{:S(2)}) %collective-permute-start.2) | collective-permute-done | bytes 131104 | tf_op jit(solution)/shard_map/ppermute | solution.py:245
  11.1 7.2 %collective-permute-done.3.refs_3_.refs_7_ = bf16[16,4096]{1,0:T(8,128)(2,1)S(1)} collective-permute-done((bf16[16,4096]{1,0:T(8,128)(2,1)S(1)}, bf16[16,4096]{1,0:T(8,128)(2,1)S(1)}, u32[]{:S(2)}, u32[]{:S(2)}) %collective-permute-start.3) | collective-permute-done | bytes 131104 | tf_op jit(solution)/shard_map/ppermute | solution.py:245
  18.3 0.0 collective-permute-done.4.refs_4_.refs_8_
  18.3 1.6 %collective-permute-start.6 = (bf16[48,4096]{1,0:T(8,128)(2,1)S(1)}, bf16[48,4096]{1,0:T(8,128)(2,1)S(1)}, u32[]{:S(2)}, u32[]{:S(2)}) collective-permute-start(bf16[48,4096]{1,0:T(8,128)(2,1)S(1)} %pad_maximum_fusion), channel_id=1, source_target_pairs={{0,2},{1,3},{2,0},{3,1},{4,6},{5,7},{6,4},{7,5},{8,10},{9,11},{10,... | collective-permute-start | bytes 1179656 | tf_op jit(solution)/shard_map/ppermute | solution.py:245
  19.9 1.7 %constant_dynamic-slice_fusion = (bf16[1024,512]{1,0:T(8,128)(2,1)S(1)}, bf16[1024,512]{1,0:T(8,128)(2,1)S(1)}) fusion(bf16[1024,1024]{1,0:T(8,128)(2,1)} %k_ref.1, s32[]{:T(128)S(6)} %select_n.37, s32[]{:T(128)S(6)} %select_n.36), kind=kLoop, calls=%fused_computation.6 | loop fusion | bytes 4194312 | tf_op jit(solution)/shard_map/dynamic_slice | solution.py:248
  21.6 0.1 collective-permute-start.5
  21.6 0.6 collective-permute-start.1
  22.2 6.7 %collective-permute-done.6 = bf16[48,4096]{1,0:T(8,128)(2,1)S(1)} collective-permute-done((bf16[48,4096]{1,0:T(8,128)(2,1)S(1)}, bf16[48,4096]{1,0:T(8,128)(2,1)S(1)}, u32[]{:S(2)}, u32[]{:S(2)}) %collective-permute-start.6) | collective-permute-done | bytes 393248 | tf_op jit(solution)/shard_map/ppermute | solution.py:245
  28.9 1.4 %collective-permute-done.1.refs_1_.refs_5_ = bf16[16,4096]{1,0:T(8,128)(2,1)S(1)} collective-permute-done((bf16[16,4096]{1,0:T(8,128)(2,1)S(1)}, bf16[16,4096]{1,0:T(8,128)(2,1)S(1)}, u32[]{:S(2)}, u32[]{:S(2)}) %collective-permute-start.1) | collective-permute-done | bytes 131104 | tf_op jit(solution)/shard_map/ppermute | solution.py:245
  30.3 0.0 collective-permute-done.5.refs_6_.refs_13_
  30.3 5.4 %early_stats.1.refs_1_ = f32[5,4,128]{2,1,0:T(4,128)S(1)} custom-call(bf16[16,4096]{1,0:T(8,128)(2,1)S(1)} %pad_maximum_fusion.1.refs_0_.refs_4_, bf16[16,4096]{1,0:T(8,128)(2,1)S(1)} %collective-permute-done.1.refs_1_.refs_5_, bf16[16,4096]{1,0:T(8,128)(2,1)S(1)} %collective-permute-done.2.refs_2_.refs_6_, ...), custom_call_target="tpu_custom_call" | custom-call | tf_op jit(solution)/shard_map/early_stats/pallas_call | solution.py:296
  35.6 0.0 copy-start.3
  35.6 0.0 copy-start.4
  35.7 3.6 %late_stats.1 = f32[8,8,4,128]{3,2,1,0:T(4,128)} custom-call(s32[1]{0:T(128)} %bitcast.refs_0_, f32[5,4,128]{2,1,0:T(4,128)S(1)} %early_stats.1.refs_1_, bf16[16,4096]{1,0:T(8,128)(2,1)S(1)} %get-tuple-element.17.refs_2_.refs_9_, bf16[16,4096]{1,0:T(8,128)(2,1)S(1)} %get-tuple-element.16.refs_3_.refs_10_, ...), custom_call_target="tpu_custom_call" | custom-call | tf_op jit(solution)/shard_map/late_stats/pallas_call | solution.py:305
  39.3 6.5 %all-to-all-start = ((f32[8,8,4,128]{3,2,1,0:T(4,128)}), f32[8,8,4,128]{3,2,1,0:T(4,128)S(1)}, u32[]{:S(2)}, u32[]{:S(2)}) async-start(f32[8,8,4,128]{3,2,1,0:T(4,128)} %late_stats.1), calls=%async_computation | async-start | bytes 262144 | tf_op jit(solution)/shard_map/all_to_all | solution.py:314
  45.8 0.0 copy-done.3
  45.8 0.0 copy-done.4
  46.5 0.0 copy-start
  46.5 1.6 %copy-done = bf16[1024,1024]{1,0:T(8,128)(2,1)S(1)} copy-done((bf16[1024,1024]{1,0:T(8,128)(2,1)S(1)}, bf16[1024,1024]{1,0:T(8,128)(2,1)}, u32[]{:S(2)}) %copy-start) | copy-done | bytes 2097176
  48.1 0.0 copy-start.1
  48.1 1.6 %copy-done.1 = bf16[1024,1024]{1,0:T(8,128)(2,1)S(1)} copy-done((bf16[1024,1024]{1,0:T(8,128)(2,1)S(1)}, bf16[1024,1024]{1,0:T(8,128)(2,1)}, u32[]{:S(2)}) %copy-start.1) | copy-done | bytes 2097176
  49.7 4.1 %compact.1 = (bf16[640,256]{1,0:T(8,128)(2,1)S(1)}, f32[8,640]{1,0:T(8,128)S(1)}) custom-call(s32[1]{0:T(128)S(6)} %copy.10.count_ref, s32[1,640]{1,0:T(1,128)S(1)} %reshape.30.entry_ref, s32[1,640]{1,0:T(1,128)S(1)} %reshape.31.owner_ref, bf16[1024,1024]{1,0:T(8,128)(2,1)S(1)} %copy-done, bf16[1024,1024]{1,0:T(8,128)(2,1)S(1)} %copy-done.1), custom_call_target="tpu_custom_call" | custom-call | tf_op jit(solution)/shard_map/compact/pallas_call | solution.py:276
  53.8 0.0 copy-start.2
  53.8 0.7 copy-done.2
  54.5 0.0 all-to-all-done.refs_1_
  54.5 6.1 %all-to-all-start.1 = ((bf16[16,40,256]{2,1,0:T(8,128)(2,1)}), bf16[16,40,256]{2,1,0:T(8,128)(2,1)}, u32[]{:S(2)}, u32[]{:S(2)}) async-start(bf16[16,40,256]{2,1,0:T(8,128)(2,1)} %bitcast.4), calls=%async_computation.1 | async-start | bytes 655360 | tf_op jit(solution)/shard_map/all_to_all | solution.py:288
  60.7 0.8 slice_select_fusion
  61.5 0.7 collective-permute-start.8
  62.1 0.0 collective-permute-done.8.refs_14_
  62.1 5.5 %collective-permute-start.9 = (bf16[16,1024]{1,0:T(8,128)(2,1)S(1)}, bf16[16,1024]{1,0:T(8,128)(2,1)S(1)}, u32[]{:S(2)}, u32[]{:S(2)}) collective-permute-start(bf16[16,1024]{1,0:T(8,128)(2,1)S(1)} %collective-permute-done.8.refs_14_), channel_id=1, source_target_pairs={{0,1},{1,0},{2,3},{3,2},{4,5},{5,4},{6,7},{7,6},{8,9},{9,8},{10,11... | collective-permute-start | bytes 98312 | tf_op jit(solution)/shard_map/ppermute | solution.py:245
  67.7 0.0 collective-permute-start.7
  67.7 1.2 %collective-permute-done.7.refs_3_ = f32[8,640]{1,0:T(8,128)S(1)} collective-permute-done((f32[8,640]{1,0:T(8,128)S(1)}, f32[8,640]{1,0:T(8,128)S(1)}, u32[]{:S(2)}, u32[]{:S(2)}) %collective-permute-start.7) | collective-permute-done | bytes 20512 | tf_op jit(solution)/shard_map/ppermute | solution.py:245
  68.8 0.0 collective-permute-done.9.refs_15_
  68.8 13.2 %mass.1 = (f32[4,1024]{1,0:T(4,128)S(1)}, f32[4,1024]{1,0:T(4,128)S(1)}, f32[16,2,128]{2,1,0:T(2,128)}) custom-call(s32[1]{0:T(128)} %bitcast.refs_0_, f32[8,8,4,128]{3,2,1,0:T(4,128)S(1)} %all-to-all-done.refs_1_, f32[8,640]{1,0:T(8,128)S(1)} %get-tuple-element.8.refs_2_, f32[8,640]{1,0:T(8,128)S(1)} %collective-permute-done.7.refs_3_, ...), custom_call_target="tpu_custom_call" | custom-call | tf_op jit(solution)/shard_map/mass/pallas_call | solution.py:324
  82.0 0.2 collective-permute-start.10
  82.2 0.0 all-to-all-done.1
  82.2 7.6 %all-to-all-start.2 = ((f32[16,2,128]{2,1,0:T(2,128)}), f32[16,2,128]{2,1,0:T(2,128)S(1)}, u32[]{:S(2)}, u32[]{:S(2)}) async-start(f32[16,2,128]{2,1,0:T(2,128)} %get-tuple-element.12), calls=%async_computation.2 | async-start | bytes 32768 | tf_op jit(solution)/shard_map/all_to_all | solution.py:338
  89.8 0.0 collective-permute-done.10
  89.8 0.6 maximum_select_fusion
  90.4 5.9 %all-to-all-done.2 = f32[16,2,128]{2,1,0:T(2,128)S(1)} async-done(((f32[16,2,128]{2,1,0:T(2,128)}), f32[16,2,128]{2,1,0:T(2,128)S(1)}, u32[]{:S(2)}, u32[]{:S(2)}) %all-to-all-start.2) | async-done | bytes 16416 | tf_op jit(solution)/shard_map/all_to_all | solution.py:338
  96.3 0.7 convert_element_type.8
  97.0 1.7 %copy.11 = bf16[640,256]{1,0:T(8,128)(2,1)} copy(bf16[640,256]{1,0:T(8,128)(2,1)} %bitcast.2) | data formatting | bytes 655360
  (7 shorter events, 0.1 us)
Async XLA Ops:
  0.6 1.7 %collective-permute-start = (bf16[8,8192]{1,0:T(8,128)(2,1)}, bf16[8,8192]{1,0:T(8,128)(2,1)S(1)}, u32[]{:S(2)}, u32[]{:S(2)}) collective-permute-start(bf16[8,8192]{1,0:T(8,128)(2,1)} %param.8), channel_id=1, source_target_pairs={{0,1},{1,0},{2,3},{3,2},{4,5},{5,4},{6,7},{7,6},{8,9},{9,8},{10,11... | collective-permute-start | bytes 393224 | tf_op jit(solution)/shard_map/ppermute | solution.py:245
  2.4 8.7 %collective-permute-start.2 = (bf16[16,4096]{1,0:T(8,128)(2,1)S(1)}, bf16[16,4096]{1,0:T(8,128)(2,1)S(1)}, u32[]{:S(2)}, u32[]{:S(2)}) collective-permute-start(bf16[16,4096]{1,0:T(8,128)(2,1)S(1)} %pad_maximum_fusion.1.refs_0_.refs_4_), channel_id=1, source_target_pairs={{0,4},{1,5},{2,6},{3,7},{4,0},{5,1},{6,2},{7,3},{8,12},{9,13},{10,... | collective-permute-start | bytes 393224 | tf_op jit(solution)/shard_map/ppermute | solution.py:245
  5.4 12.9 %collective-permute-start.3 = (bf16[16,4096]{1,0:T(8,128)(2,1)S(1)}, bf16[16,4096]{1,0:T(8,128)(2,1)S(1)}, u32[]{:S(2)}, u32[]{:S(2)}) collective-permute-start(bf16[16,4096]{1,0:T(8,128)(2,1)S(1)} %pad_maximum_fusion.1.refs_0_.refs_4_), channel_id=1, source_target_pairs={{0,8},{1,9},{2,10},{3,11},{4,12},{5,13},{6,14},{7,15},{8,0},{9,1},... | collective-permute-start | bytes 393224 | tf_op jit(solution)/shard_map/ppermute | solution.py:245
  8.0 10.3 %collective-permute-start.4 = (bf16[16,4096]{1,0:T(8,128)(2,1)S(1)}, bf16[16,4096]{1,0:T(8,128)(2,1)S(1)}, u32[]{:S(2)}, u32[]{:S(2)}) collective-permute-start(bf16[16,4096]{1,0:T(8,128)(2,1)S(1)} %pad_maximum_fusion.1.refs_0_.refs_4_), channel_id=1, source_target_pairs={{0,12},{1,13},{2,14},{3,15},{4,8},{5,9},{6,10},{7,11},{8,4},{9,5},... | collective-permute-start | bytes 393224 | tf_op jit(solution)/shard_map/ppermute | solution.py:245
  18.3 10.6 %collective-permute-start.6 = (bf16[48,4096]{1,0:T(8,128)(2,1)S(1)}, bf16[48,4096]{1,0:T(8,128)(2,1)S(1)}, u32[]{:S(2)}, u32[]{:S(2)}) collective-permute-start(bf16[48,4096]{1,0:T(8,128)(2,1)S(1)} %pad_maximum_fusion), channel_id=1, source_target_pairs={{0,2},{1,3},{2,0},{3,1},{4,6},{5,7},{6,4},{7,5},{8,10},{9,11},{10,... | collective-permute-start | bytes 1179656 | tf_op jit(solution)/shard_map/ppermute | solution.py:245
  21.6 8.7 %collective-permute-start.5 = (bf16[1024,512]{1,0:T(8,128)(2,1)S(1)}, bf16[1024,512]{1,0:T(8,128)(2,1)S(1)}, u32[]{:S(2)}, u32[]{:S(2)}) collective-permute-start(bf16[1024,512]{1,0:T(8,128)(2,1)S(1)} %get-tuple-element.13), channel_id=1, source_target_pairs={{0,1},{1,0},{2,3},{3,2},{4,5},{5,4},{6,7},{7,6},{8,9},{9,8},{10,11... | collective-permute-start | bytes 3145736 | tf_op jit(solution)/shard_map/ppermute | solution.py:245
  21.6 8.6 %collective-permute-start.1 = (bf16[16,4096]{1,0:T(8,128)(2,1)S(1)}, bf16[16,4096]{1,0:T(8,128)(2,1)S(1)}, u32[]{:S(2)}, u32[]{:S(2)}) collective-permute-start(bf16[16,4096]{1,0:T(8,128)(2,1)S(1)} %pad_maximum_fusion.1.refs_0_.refs_4_), channel_id=1, source_target_pairs={{0,2},{1,3},{2,0},{3,1},{4,6},{5,7},{6,4},{7,5},{8,10},{9,11},{10,... | collective-permute-start | bytes 393224 | tf_op jit(solution)/shard_map/ppermute | solution.py:245
  35.6 10.2 %copy-start.3 = (s32[640]{0:T(1024)S(1)}, s32[640]{0:T(1024)}, u32[]{:S(2)}) copy-start(s32[640]{0:T(1024)} %param.10) | copy-start | bytes 7684
  35.6 10.2 %copy-start.4 = (s32[640]{0:T(1024)S(1)}, s32[640]{0:T(1024)}, u32[]{:S(2)}) copy-start(s32[640]{0:T(1024)} %param.11) | copy-start | bytes 7684
  39.3 15.3 %all-to-all-start = ((f32[8,8,4,128]{3,2,1,0:T(4,128)}), f32[8,8,4,128]{3,2,1,0:T(4,128)S(1)}, u32[]{:S(2)}, u32[]{:S(2)}) async-start(f32[8,8,4,128]{3,2,1,0:T(4,128)} %late_stats.1), calls=%async_computation | async-start | bytes 262144 | tf_op jit(solution)/shard_map/all_to_all | solution.py:314
  46.5 1.6 %copy-start = (bf16[1024,1024]{1,0:T(8,128)(2,1)S(1)}, bf16[1024,1024]{1,0:T(8,128)(2,1)}, u32[]{:S(2)}) copy-start(bf16[1024,1024]{1,0:T(8,128)(2,1)} %k_ref.1) | copy-start | bytes 6291460
  48.1 1.6 %copy-start.1 = (bf16[1024,1024]{1,0:T(8,128)(2,1)S(1)}, bf16[1024,1024]{1,0:T(8,128)(2,1)}, u32[]{:S(2)}) copy-start(bf16[1024,1024]{1,0:T(8,128)(2,1)} %v_ref.1) | copy-start | bytes 6291460
  53.8 0.7 copy-start.2
  54.5 27.7 %all-to-all-start.1 = ((bf16[16,40,256]{2,1,0:T(8,128)(2,1)}), bf16[16,40,256]{2,1,0:T(8,128)(2,1)}, u32[]{:S(2)}, u32[]{:S(2)}) async-start(bf16[16,40,256]{2,1,0:T(8,128)(2,1)} %bitcast.4), calls=%async_computation.1 | async-start | bytes 655360 | tf_op jit(solution)/shard_map/all_to_all | solution.py:288
  61.5 0.7 collective-permute-start.8
  62.1 6.7 %collective-permute-start.9 = (bf16[16,1024]{1,0:T(8,128)(2,1)S(1)}, bf16[16,1024]{1,0:T(8,128)(2,1)S(1)}, u32[]{:S(2)}, u32[]{:S(2)}) collective-permute-start(bf16[16,1024]{1,0:T(8,128)(2,1)S(1)} %collective-permute-done.8.refs_14_), channel_id=1, source_target_pairs={{0,1},{1,0},{2,3},{3,2},{4,5},{5,4},{6,7},{7,6},{8,9},{9,8},{10,11... | collective-permute-start | bytes 98312 | tf_op jit(solution)/shard_map/ppermute | solution.py:245
  67.7 1.2 %collective-permute-start.7 = (f32[8,640]{1,0:T(8,128)S(1)}, f32[8,640]{1,0:T(8,128)S(1)}, u32[]{:S(2)}, u32[]{:S(2)}) collective-permute-start(f32[8,640]{1,0:T(8,128)S(1)} %get-tuple-element.8.refs_2_), channel_id=1, source_target_pairs={{0,1},{1,0},{2,3},{3,2},{4,5},{5,4},{6,7},{7,6},{8,9},{9,8},{10,11... | collective-permute-start | bytes 61448 | tf_op jit(solution)/shard_map/ppermute | solution.py:245
  82.0 7.7 %collective-permute-start.10 = (f32[4,1024]{1,0:T(4,128)S(1)}, f32[4,1024]{1,0:T(4,128)S(1)}, u32[]{:S(2)}, u32[]{:S(2)}) collective-permute-start(f32[4,1024]{1,0:T(4,128)S(1)} %get-tuple-element.10), channel_id=1, source_target_pairs={{0,1},{1,0},{2,3},{3,2},{4,5},{5,4},{6,7},{7,6},{8,9},{9,8},{10,11... | collective-permute-start | bytes 49160 | tf_op jit(solution)/shard_map/ppermute | solution.py:245
  82.2 14.1 %all-to-all-start.2 = ((f32[16,2,128]{2,1,0:T(2,128)}), f32[16,2,128]{2,1,0:T(2,128)S(1)}, u32[]{:S(2)}, u32[]{:S(2)}) async-start(f32[16,2,128]{2,1,0:T(2,128)} %get-tuple-element.12), calls=%async_computation.2 | async-start | bytes 32768 | tf_op jit(solution)/shard_map/all_to_all | solution.py:338

commit v2 on v1

v2 whole, which is shorter than its diff:
```python
import functools

import jax
import jax.numpy as jnp
from jax import lax
from jax.experimental import pallas as pl
from jax.experimental.pallas import tpu as pltpu
from jax.sharding import PartitionSpec as P

HEADS = 64
KV_HEADS = 8
HEAD_DIM = 128
GROUP = 8
WINDOW = 128
POOL = 7
HALF = KV_HEADS // 2
EDGE = 16
SCALE2 = HEAD_DIM ** (-0.5) * 1.4426950408889634
MIB = 1 << 20

VMEM = pl.BlockSpec(memory_space=pltpu.VMEM)
SMEM = pl.BlockSpec(memory_space=pltpu.SMEM)
ANYWHERE = pl.BlockSpec(memory_space=pl.ANY)
GRANT = 56 * MIB


def nt(a, b, precision=None):
    return lax.dot_general(
        a, b, (((1,), (1,)), ((), ())), precision=precision, preferred_element_type=jnp.float32
    )


def one_hot(mask):
    return jnp.where(mask, 1.0, 0.0).astype(jnp.bfloat16)


def iota(shape, dim):
    return lax.broadcasted_iota(jnp.int32, shape, dim)


def compact_kernel(
    peers, count_ref, entry_ref, owner_ref, k_source, v_source, rows_ref, code_ref, k_ref, v_ref, sems
):
    copies = (
        pltpu.make_async_copy(k_source, k_ref, sems.at[0]),
        pltpu.make_async_copy(v_source, v_ref, sems.at[1]),
    )
    for copy in copies:
        copy.start()
    positions = k_ref.shape[0]
    slots = entry_ref.shape[1]
    capacity = slots // peers
    owner, entry = owner_ref[...], entry_ref[...]
    live = iota((1, slots), 1) < count_ref[0]
    member = jnp.where((owner == iota((peers, slots), 0)) & live, 1.0, 0.0)
    before = one_hot(iota((slots, slots), 0) < iota((slots, slots), 1))
    earlier = jnp.dot(member.astype(jnp.bfloat16), before, preferred_element_type=jnp.float32)
    rank = jnp.sum(earlier * member, axis=0, keepdims=True).astype(jnp.int32)
    target = jnp.where(live, owner * capacity + rank, -1)
    placed = one_hot(iota((slots, slots), 0) == target)
    token, head = entry % positions, entry // positions
    line = iota((8, slots), 0)
    facts = jnp.where(
        line == 0, 1, jnp.where(line == 1, head, jnp.where(line == 2, token // 64, token % 64))
    )
    facts = facts.astype(jnp.float32).astype(jnp.bfloat16)
    by_row = nt(facts, placed)
    row_token = jnp.where(by_row[0:1] > 0.5, by_row[2:3] * 64 + by_row[3:4], -1.0)
    code_ref[...] = jnp.where(iota((8, slots), 0) == 0, row_token, by_row[1:2])
    by_col = nt(placed, facts)
    col_head = by_col[:, 1:2].astype(jnp.int32)
    col_token = jnp.where(by_col[:, 0:1] > 0.5, by_col[:, 2:3] * 64 + by_col[:, 3:4], -1.0)
    col_token = col_token.astype(jnp.int32)
    step = 128 if slots % 128 == 0 else slots
    for side, source in enumerate((k_ref, v_ref)):
        copies[side].wait()
        for start in range(0, slots, step):
            token_part = col_token[start : start + step]
            head_part = col_head[start : start + step]
            pick = one_hot(iota((step, positions), 1) == token_part)
            found = jnp.dot(pick, source[...], preferred_element_type=jnp.float32)
            kept = jnp.zeros((step, HEAD_DIM), jnp.float32)
            for g in range(KV_HEADS):
                part = found[:, g * HEAD_DIM : (g + 1) * HEAD_DIM]
                kept = kept + jnp.where(head_part == g, part, 0.0)
            rows_ref[start : start + step, side * HEAD_DIM : (side + 1) * HEAD_DIM] = kept.astype(
                jnp.bfloat16
            )


def query_rows(block_refs, g):
    parts = []
    for ref in block_refs:
        for h in range(GROUP):
            first = (g * GROUP + h) * HEAD_DIM
            parts.append(ref[:, first : first + HEAD_DIM])
    return jnp.concatenate(parts, axis=0)


def spread(limits, value):
    low, high = limits
    return jnp.minimum(low, jnp.min(value)), jnp.maximum(high, jnp.max(value))


def fetch_keys(sources, held, sems):
    copies = []
    for g in range(HALF):
        for i, source in enumerate(sources):
            cols = slice(g * HEAD_DIM, (g + 1) * HEAD_DIM)
            copies.append(pltpu.make_async_copy(source.at[:, cols], held.at[g, i], sems.at[g, i]))
    for copy in copies:
        copy.start()

    def wait(g):
        for copy in copies[2 * g : 2 * g + 2]:
            copy.wait()

    return wait


def local_stats(block_refs, k_refs, store):
    per_block = GROUP * block_refs[0].shape[0]
    tokens = k_refs[0].shape[0]

    def keep(g, lse):
        for b in range(len(block_refs)):
            store(b, g, lse[:, b * per_block : (b + 1) * per_block])

    limits = (jnp.float32(jnp.inf), jnp.float32(-jnp.inf))
    step = min(512, tokens)
    for g in range(HALF):
        rows = query_rows(block_refs, g)
        count = rows.shape[0]
        total = jnp.zeros((8, count), jnp.float32)
        cols = slice(g * HEAD_DIM, (g + 1) * HEAD_DIM)
        for k_ref in k_refs:
            for start in range(0, tokens, step):
                weights = jnp.exp2(nt(k_ref[start : start + step, cols], rows) * SCALE2)
                total = total + jnp.sum(weights.reshape(step // 8, 8, count), axis=0)
        total = jnp.sum(total, axis=0, keepdims=True)
        limits = spread(limits, total)
        keep(g, jnp.log2(total))

    in_range = (limits[0] > 2.0**-60) & (limits[1] < 2.0**100)

    @pl.when(jnp.logical_not(in_range))
    def _():
        part = min(256, tokens)
        for g in range(HALF):
            rows = query_rows(block_refs, g)
            count = rows.shape[0]
            carry = (jnp.full((1, count), -jnp.inf, jnp.float32), jnp.zeros((1, count), jnp.float32))
            cols = slice(g * HEAD_DIM, (g + 1) * HEAD_DIM)
            for k_ref in k_refs:

                def advance(j, carry):
                    peak, total = carry
                    start = pl.multiple_of(j * part, part)
                    scores = nt(k_ref[pl.ds(start, part), cols], rows)
                    higher = jnp.maximum(peak, jnp.max(scores, axis=0, keepdims=True))
                    total = total * jnp.exp2((peak - higher) * SCALE2) + jnp.sum(
                        jnp.exp2((scores - higher) * SCALE2), axis=0, keepdims=True
                    )
                    return higher, total

                carry = lax.fori_loop(0, tokens // part, advance, carry)
            keep(g, carry[0] * SCALE2 + jnp.log2(carry[1]))


def sender(chip, offset):
    return 0 if offset is None else chip ^ offset


def fetch(sources, held, sems):
    copies = [pltpu.make_async_copy(x, held.at[i], sems.at[i]) for i, x in enumerate(sources)]
    for copy in copies:
        copy.start()
    return copies


def early_stats_kernel(count, *refs):
    blocks, k_refs, out_ref = refs[:count], refs[count : count + 2], refs[-1]

    def store(b, g, lse):
        out_ref[b, g : g + 1, :] = lse

    local_stats(blocks, k_refs, store)


def stats_kernel(offsets, early, dests, *refs):
    place_ref, k_refs = refs[0], refs[1:3]
    out_ref, hold = refs[-2:]
    chip = place_ref[0] // 2
    done = 0
    for ref, size in zip(refs[3:], early):
        for b in range(size):
            hold[sender(chip, offsets[done + b])] = ref[b]
        done += size

    def store(b, g, lse):
        hold[sender(chip, offsets[done + b]), g : g + 1, :] = lse

    local_stats(refs[3 + len(early) : -2], k_refs, store)
    everything = hold[...]
    for d in range(dests):
        out_ref[d] = everything


def fetch(sources, held, sems):
    copies = [pltpu.make_async_copy(x, held.at[i], sems.at[i]) for i, x in enumerate(sources)]
    for copy in copies:
        copy.start()
    return copies


def split3(x):
    high = x.astype(jnp.bfloat16)
    rest = x - high.astype(jnp.float32)
    middle = rest.astype(jnp.bfloat16)
    low = (rest - middle.astype(jnp.float32)).astype(jnp.bfloat16)
    return high, middle, low


def mass_kernel(offsets, peers, factor, width, edges, *refs):
    count = len(offsets)
    place_ref, stats_ref, k_own, k_sib = refs[:4]
    code_sources = refs[4:6]
    edge_refs, refs = refs[6 : 6 + edges], refs[6 + edges :]
    sources = refs[:count]
    imp_own, imp_sib, score_ref = refs[count : count + 3]
    lse_ref, side_ref, blocks_held, held, codes, block_sems, sems, code_sems = refs[count + 3 :]
    copies = fetch(sources, blocks_held, block_sems)
    wait = fetch_keys((k_own, k_sib), held, sems)
    code_copies = fetch(code_sources, codes, code_sems)
    blocks = [blocks_held.at[i] for i in range(count)]
    tokens = held.shape[2]
    core = place_ref[0] % 2
    chip = place_ref[0] // 2
    chips = peers // 2
    is_low = core == 0

    stats = stats_ref[...]
    top = jnp.max(stats, axis=0)
    lse_ref[...] = top + jnp.log2(jnp.sum(jnp.exp2(stats - top[None]), axis=0))

    for copy in copies:
        copy.wait()
    step = min(512, tokens)
    found = [[], []]
    rims = []
    for g in range(HALF):
        rows = query_rows(blocks, g)
        lse = jnp.concatenate([lse_ref[sender(chip, off), g : g + 1, :] for off in offsets], axis=1)
        parts = jnp.concatenate(
            split3(lse) + (jnp.zeros((5, lse.shape[1]), jnp.bfloat16),), axis=0
        )
        side_ref[...] = lax.dot_general(
            parts, jnp.ones((8, HEAD_DIM), jnp.bfloat16), (((0,), (0,)), ((), ())),
            preferred_element_type=jnp.float32,
        )
        wait(g)
        for i in range(2):
            line = []
            for start in range(0, tokens, step):
                shift = jnp.concatenate([side_ref[...]] * (step // HEAD_DIM), axis=1)
                weights = jnp.exp2(nt(rows, held[g, i, start : start + step, :]) * SCALE2 - shift)
                line.append(jnp.sum(weights, axis=0, keepdims=True))
            found[i].append(jnp.concatenate(line, axis=1))
        if edges:
            low = slice(g * HEAD_DIM, (g + 1) * HEAD_DIM)
            high = slice((HALF + g) * HEAD_DIM, (HALF + g + 1) * HEAD_DIM)
            rim_keys = [jnp.where(is_low, ref[:, low], ref[:, high]) for ref in edge_refs]
        else:
            cols = slice(width + g * HEAD_DIM, width + (g + 1) * HEAD_DIM)
            rim_keys = []
            for other in (chip ^ jnp.maximum(chip - 1, 0), chip ^ jnp.minimum(chip + 1, chips - 1)):
                where = sum(jnp.where(other == off, i, 0) for i, off in enumerate(offsets))
                rim_keys.append(blocks_held[where, :, cols])
        weights = jnp.exp2(nt(jnp.concatenate(rim_keys, axis=0), rows) * SCALE2 - lse)
        folded = weights[:, 0:HEAD_DIM]
        for first in range(HEAD_DIM, weights.shape[1], HEAD_DIM):
            folded = folded + weights[:, first : first + HEAD_DIM]
        rims.append(jnp.sum(folded.T, axis=0, keepdims=True))
    own = jnp.concatenate(found[0], axis=0)
    sib = jnp.concatenate(found[1], axis=0)
    rim = jnp.concatenate(rims, axis=0)
    first = jnp.where(is_low, own, sib)
    second = jnp.where(is_low, sib, own)
    side = POOL // 2
    if edges:
        rim_own, rim_sib = rim[:, :EDGE], rim[:, EDGE : 2 * EDGE]
        before = jnp.where(is_low, rim_own, rim_sib)[:, EDGE - side :]
        after = jnp.where(is_low, rim_sib, rim_own)[:, :side]
    else:
        size = blocks_held.shape[1]
        mid = size // 2
        before = jnp.where(is_low, rim[:, size - side : size], rim[:, mid - side : mid])
        after = jnp.where(is_low, rim[:, size : size + side], rim[:, size + mid : size + mid + side])
    before = jnp.where(chip == 0, 0.0, before)
    after = jnp.where(chip == chips - 1, 0.0, after)
    padded = jnp.concatenate([before, first, second, after], axis=1)
    pooled = padded[:, 0 : 2 * tokens]
    for shift in range(1, POOL):
        pooled = pooled + padded[:, shift : shift + 2 * tokens]
    importance = pooled * factor
    halves = (importance[:, :tokens], importance[:, tokens:])
    imp_own[...] = jnp.where(is_low, halves[0], halves[1])
    imp_sib[...] = jnp.where(is_low, halves[1], halves[0])
    for copy in code_copies:
        copy.wait()
    slots = codes.shape[2]
    capacity = slots // peers
    for side in range(2):
        code = jnp.where(core == side, codes[0], codes[1]).astype(jnp.int32)
        parts = jnp.concatenate(split3(halves[side]), axis=0)
        pick = one_hot(iota((tokens, slots), 0) == code[0:1])
        hits = jnp.dot(parts, pick, preferred_element_type=jnp.float32)
        value = hits[0:HALF] + hits[HALF : 2 * HALF] + hits[2 * HALF : 3 * HALF]
        mine = iota((HALF, slots), 0) + core * HALF == code[1:2]
        score = jnp.sum(jnp.where(mine, value, 0.0), axis=0, keepdims=True)
        for p in range(peers):
            score_ref[p, side : side + 1, 0:capacity] = score[:, p * capacity : (p + 1) * capacity]


def after(x, *earlier):
    return lax.optimization_barrier((x, earlier))[0]


def per_device(cached_keys, cached_values, window_queries, kept_count, kept_entry, row_owner):
    positions = cached_keys.shape[0]
    peers = lax.axis_size("seq")
    chips = peers // 2
    slots = kept_entry.shape[0]
    capacity = slots // peers
    me = lax.axis_index("seq")
    core = me % 2
    place = me.astype(jnp.int32).reshape(1)
    half_keys = HALF * HEAD_DIM
    half_queries = HALF * GROUP * HEAD_DIM

    def swap(x, distance):
        return lax.ppermute(x, "seq", [(i, i ^ distance) for i in range(peers)])

    def half(x, which, width):
        return lax.dynamic_slice_in_dim(x, which * width, width, axis=1)

    def joined(parts):
        return jnp.concatenate(parts, axis=0)

    lines = chips // 2
    shard_rows = window_queries.shape[0]
    stepwise = shard_rows % 8 == 0 and chips % 4 == 0 and lines & (lines - 1) == 0
    edge = shard_rows if stepwise else EDGE
    rim = jnp.where(core == 1, cached_keys[positions - edge :], cached_keys[:edge])
    sibling_queries = swap(window_queries, 1)
    pair = [half(window_queries, core, half_queries), half(sibling_queries, core, half_queries)]
    if stepwise:
        sibling_rim = swap(rim, 1)
        ends = [half(rim, core, half_keys), half(sibling_rim, core, half_keys)]
        piece = joined([jnp.concatenate(x, axis=1) for x in zip(pair, ends)])
        edges = []
    else:
        piece = joined(pair)
        offsets = [None]
        ring = [(2 * i + 1, 2 * i + 2) for i in range(chips - 1)]
        edge_own = lax.ppermute(rim, "seq", ring + [(b, a) for a, b in ring])
        edges = [edge_own, swap(edge_own, 1)]

    def keys_held():
        return [
            pltpu.VMEM((HALF, 2, positions, HEAD_DIM), jnp.bfloat16),
            pltpu.SemaphoreType.DMA((HALF, 2)),
        ]

    def blocks_held(some):
        return [
            pltpu.VMEM((len(some),) + some[0].shape, jnp.bfloat16),
            pltpu.SemaphoreType.DMA((len(some),)),
        ]

    def score_cost(some):
        queries = len(some) * HALF * GROUP * some[0].shape[0]
        return pl.CostEstimate(
            flops=4 * queries * positions * HEAD_DIM,
            bytes_accessed=2 * positions * half_keys,
            transcendentals=0,
        )

    def early_stats(some):
        shape = (len(some), HALF, GROUP * some[0].shape[0])
        return pl.pallas_call(
            functools.partial(early_stats_kernel, len(some)),
            out_shape=jax.ShapeDtypeStruct(shape, jnp.float32),
            in_specs=[VMEM] * (len(some) + 2),
            out_specs=VMEM,
            compiler_params=pltpu.CompilerParams(vmem_limit_bytes=8 * MIB),
            cost_estimate=score_cost(some),
            name="early_stats",
        )(*some, k_own, k_sib)

    if stepwise:
        line, distance = [(0, piece)], lines // 2
        while distance:
            for off, block in list(line):
                if distance == 1 and off == 0:
                    near = swap(block, 4)
                    line.append((2, near))
                else:
                    if distance == 1:
                        block = after(block, near)
                    line.append((off ^ 2 * distance, swap(block, 4 * distance)))
            distance //= 2
        beside = {off: swap(block, 2) for off, block in line[:-1]}
        start = [(0, piece), (1, beside[0]), (2, near), (3, beside[2])]
        sets = [start]
        for off, block in line[:-1]:
            if off not in (0, 2):
                sets.append([(off, block), (off ^ 1, beside[off])])
        final = line[-1]
        ready_keys = after(cached_keys, piece)
    else:
        same_core = [[i for i in range(peers) if i % 2 == c] for c in range(2)]
        gathered = lax.all_gather(piece, "seq", axis=0, tiled=True, axis_index_groups=same_core)
        sets, final = [], (None, gathered)
        ready_keys = after(cached_keys, piece)

    k_own = half(ready_keys, core, half_keys)
    k_sib = swap(half(ready_keys, 1 - core, half_keys), 1)

    first = [early_stats([block for _, block in some]) for some in sets]
    if stepwise:
        off, block = final
        sets.append([final, (off ^ 1, swap(after(block, beside[2]), 2))])
    else:
        sets.append([final])
    blocks = [block for some in sets for _, block in some]
    offsets = [off for some in sets for off, _ in some]
    late = [block for _, block in sets[-1]]
    count = len(offsets)
    per_block = GROUP * blocks[0].shape[0]
    sent = pl.pallas_call(
        functools.partial(stats_kernel, offsets, [x.shape[0] for x in first], chips),
        out_shape=jax.ShapeDtypeStruct((chips, count, HALF, per_block), jnp.float32),
        in_specs=[SMEM] + [VMEM] * (2 + len(first) + len(late)),
        out_specs=VMEM,
        scratch_shapes=[pltpu.VMEM((count, HALF, per_block), jnp.float32)],
        compiler_params=pltpu.CompilerParams(vmem_limit_bytes=8 * MIB),
        cost_estimate=score_cost(late),
        name="late_stats",
    )(place, k_own, k_sib, *first, *late)

    rows_out, code_own = pl.pallas_call(
        functools.partial(compact_kernel, peers),
        out_shape=(
            jax.ShapeDtypeStruct((slots, 2 * HEAD_DIM), jnp.bfloat16),
            jax.ShapeDtypeStruct((8, slots), jnp.float32),
        ),
        in_specs=[SMEM, VMEM, VMEM, ANYWHERE, ANYWHERE],
        out_specs=(VMEM, VMEM),
        scratch_shapes=[
            pltpu.VMEM(cached_keys.shape, jnp.bfloat16),
            pltpu.VMEM(cached_values.shape, jnp.bfloat16),
            pltpu.SemaphoreType.DMA((2,)),
        ],
        compiler_params=pltpu.CompilerParams(vmem_limit_bytes=GRANT),
        cost_estimate=pl.CostEstimate(
            flops=4 * slots * positions * KV_HEADS * HEAD_DIM,
            bytes_accessed=4 * positions * KV_HEADS * HEAD_DIM,
            transcendentals=0,
        ),
        name="compact",
    )(
        kept_count,
        after(kept_entry, sent).reshape(1, slots),
        row_owner.reshape(1, slots),
        cached_keys,
        cached_values,
    )
    code_sib = swap(code_own, 1)
    got_rows = lax.all_to_all(
        rows_out.reshape(peers, capacity, 2 * HEAD_DIM), "seq", split_axis=0, concat_axis=0, tiled=True
    ).reshape(slots, 2 * HEAD_DIM)

    stats = lax.all_to_all(
        sent,
        "seq",
        split_axis=0,
        concat_axis=0,
        tiled=True,
        axis_index_groups=[[i for i in range(peers) if i % 2 == c] for c in range(2)],
    )
    factor = peers * positions / (GROUP * WINDOW * POOL)
    imp_own, imp_sib, score = pl.pallas_call(
        functools.partial(mass_kernel, offsets, peers, factor, half_queries, len(edges)),
        out_shape=(
            jax.ShapeDtypeStruct((HALF, positions), jnp.float32),
            jax.ShapeDtypeStruct((HALF, positions), jnp.float32),
            jax.ShapeDtypeStruct((peers, 2, 128), jnp.float32),
        ),
        in_specs=[SMEM, VMEM] + [ANYWHERE] * 4 + [VMEM] * len(edges) + [ANYWHERE] * count,
        out_specs=(VMEM, VMEM, VMEM),
        scratch_shapes=[
            pltpu.VMEM((count, HALF, per_block), jnp.float32),
            pltpu.VMEM((count * per_block, HEAD_DIM), jnp.float32),
            blocks_held(blocks)[0],
            keys_held()[0],
            pltpu.VMEM((2, 8, slots), jnp.float32),
            blocks_held(blocks)[1],
            keys_held()[1],
            pltpu.SemaphoreType.DMA((2,)),
        ],
        compiler_params=pltpu.CompilerParams(vmem_limit_bytes=GRANT),
        cost_estimate=score_cost(blocks),
        name="mass",
    )(place, stats, k_own, k_sib, code_own, code_sib, *edges, *blocks)

    got_score = lax.all_to_all(after(score, got_rows), "seq", split_axis=0, concat_axis=0, tiled=True)
    by_core = got_score.reshape(chips, 2, 2, 128)[..., :capacity]
    score_out = (by_core[:, 0] + by_core[:, 1]).astype(jnp.bfloat16)
    imp_other = swap(imp_sib, 1)
    importance = jnp.where(
        core == 0,
        jnp.concatenate([imp_own, imp_other], axis=0),
        jnp.concatenate([imp_other, imp_own], axis=0),
    )
    return (
        importance,
        got_rows,
        score_out.reshape(peers * capacity),
    )


def solution(mesh):
    in_specs = (
        P(("rep", "seq"), None),
        P(("rep", "seq"), None),
        P(("rep", "seq"), None),
        P(("rep", "seq")),
        P(("rep", "seq")),
        P(("rep", "seq")),
    )
    out_specs = (P("rep", "seq"), P(("rep", "seq"), None), P(("rep", "seq")))
    return jax.shard_map(
        per_device, mesh=mesh, in_specs=in_specs, out_specs=out_specs, check_vma=False
    )
```

time: 99.3 us -> 104 us (1.047); the launches traced: 98.7 us -> 105 us
  Pallas kernels: 26.3 us -> 42.9 us
  waiting for transfers between devices: 25.7 us -> 17.3 us
  local copies, waits for them, and re-layouts: 8.86 us -> 5.83 us
    pallas_call x3 -> x4, Pallas kernels: 22.1 us -> 36.5 us  [the longest x2 23.6 us: early_stats(): pl.pallas_call(functools.partial(early_stats_kernel, len(some)), out_shap...]
    ppermute x10 -> x12, waiting for transfers between devices: 19.9 us -> 11.8 us  [swap(): return lax.ppermute(x, 'seq', [(i, i ^ distance) for i in range(peers)])]
    all_to_all x1, starting transfers between devices: 6.54 us -> 11.3 us  [per_device(): lax.all_to_all(sent, 'seq', split_axis=0, concat_axis=0, tiled=True, axis...]
    unnamed x11 -> x29, local copies, waits for them, and re-layouts: 5.62 us -> 1.38 us
    pallas_call x1, Pallas kernels: 4.11 us -> 6.36 us  [per_device(): pl.pallas_call(functools.partial(compact_kernel, peers), out_shape=(jax.S...]
    all_to_all x1, starting transfers between devices: 7.57 us -> 5.76 us  [per_device(): lax.all_to_all(after(score, got_rows), 'seq', split_axis=0, concat_axis=0...]
    ppermute x10 -> x12, starting transfers between devices: 14 us -> 12.7 us  [swap(): return lax.ppermute(x, 'seq', [(i, i ^ distance) for i in range(peers)])]
    dynamic_slice x3 -> x5, local copies, waits for them, and re-layouts: 2.52 us -> 2.6 us  [half(): return lax.dynamic_slice_in_dim(x, which * width, width, axis=1)]
  transfers between devices with their start and end apart: 14 -> 15, of which waited for: 7 -> 8; matrix products, arithmetic and copies ran while one was open for 4% -> 3% of each run, Pallas kernels for 18% -> 39%
where the time goes in v2:
time: 104 us; the launch traced here: 105 us
  Pallas kernels  42.9 us (41%)
  starting transfers between devices  35.5 us (34%)
  waiting for transfers between devices  17.3 us (17%)
  local copies, waits for them, and re-layouts  5.83 us (6%)
  other arithmetic  2.19 us (2%)
  between operations  1.52 us (1%)
    pallas_call x2, Pallas kernels, early_stats(): pl.pallas_call(functools.partial(early_stats_kernel, len(some)), out_shap...  23.6 us
    ppermute x12, starting transfers between devices, swap(): return lax.ppermute(x, 'seq', [(i, i ^ distance) for i in range(peers)])  12.7 us
    ppermute x12, waiting for transfers between devices, swap(): return lax.ppermute(x, 'seq', [(i, i ^ distance) for i in range(peers)])  11.8 us
    all_to_all x1, starting transfers between devices, per_device(): lax.all_to_all(sent, 'seq', split_axis=0, concat_axis=0, tiled=True, axis...  11.3 us
    pallas_call x1, Pallas kernels, per_device(): pl.pallas_call(functools.partial(mass_kernel, offsets, peers, factor, hal...  10.8 us
    pallas_call x1, Pallas kernels, per_device(): pl.pallas_call(functools.partial(compact_kernel, peers), out_shape=(jax.S...  6.36 us
    all_to_all x1, starting transfers between devices, per_device(): lax.all_to_all(after(score, got_rows), 'seq', split_axis=0, concat_axis=0...  5.76 us
    all_to_all x1, starting transfers between devices, per_device(): lax.all_to_all(rows_out.reshape(peers, capacity, 2 * HEAD_DIM), 'seq', sp...  5.75 us
  transfers between devices with their start and end apart: 15, of which 8 were waited for; matrix products, arithmetic and copies ran while one was open for 3% of the time, Pallas kernels for 39%

profile of v2, /device:TPU:0, one launch (start us, length us, event | category | flops | bytes accessed | tf_op | source)
XLA Modules:
  0.0 105.2 jit_solution(11658743166385530869)
XLA Ops:
  0.6 0.7 slice_select_fusion
  1.4 0.5 collective-permute-start.1
  1.8 0.1 collective-permute-start
  1.9 0.8 constant_dynamic-slice_fusion.5
  2.7 0.0 collective-permute-done.1
  2.8 0.6 collective-permute-done
  3.4 0.0 copy-start.11
  3.4 1.7 %constant_dynamic-slice_fusion = (bf16[1024,512]{1,0:T(8,128)(2,1)S(1)}, bf16[1024,512]{1,0:T(8,128)(2,1)S(1)}) fusion(bf16[1024,1024]{1,0:T(8,128)(2,1)} %k_source.1, s32[]{:T(128)S(6)} %select_n.41, s32[]{:T(128)S(6)} %select_n.40), kind=kLoop, calls=%fused_computation.5 | loop fusion | bytes 4194312 | tf_op jit(solution)/shard_map/dynamic_slice | solution.py:345
  5.2 0.0 copy-start
  5.2 0.2 collective-permute-start.2
  5.4 2.9 %collective-permute-start.4 = (bf16[16,4608]{1,0:T(8,128)(2,1)S(1)}, bf16[16,4608]{1,0:T(8,128)(2,1)S(1)}, u32[]{:S(2)}, u32[]{:S(2)}) collective-permute-start(bf16[16,4608]{1,0:T(8,128)(2,1)S(1)} %maximum_maximum_fusion.refs_0_.refs_6_), channel_id=1, source_target_pairs={{0,4},{1,5},{2,6},{3,7},{4,0},{5,1},{6,2},{7,3},{8,12},{9,13},{10,... | collective-permute-start | bytes 442376 | tf_op jit(solution)/shard_map/ppermute | solution.py:342
  8.3 2.6 %collective-permute-start.6 = (bf16[16,4608]{1,0:T(8,128)(2,1)S(1)}, bf16[16,4608]{1,0:T(8,128)(2,1)S(1)}, u32[]{:S(2)}, u32[]{:S(2)}) collective-permute-start(bf16[16,4608]{1,0:T(8,128)(2,1)S(1)} %maximum_maximum_fusion.refs_0_.refs_6_), channel_id=1, source_target_pairs={{0,8},{1,9},{2,10},{3,11},{4,12},{5,13},{6,14},{7,15},{8,0},{9,1},... | collective-permute-start | bytes 442376 | tf_op jit(solution)/shard_map/ppermute | solution.py:342
  10.9 4.5 %collective-permute-done.4.refs_2_.refs_8_ = bf16[16,4608]{1,0:T(8,128)(2,1)S(1)} collective-permute-done((bf16[16,4608]{1,0:T(8,128)(2,1)S(1)}, bf16[16,4608]{1,0:T(8,128)(2,1)S(1)}, u32[]{:S(2)}, u32[]{:S(2)}) %collective-permute-start.4) | collective-permute-done | bytes 147488 | tf_op jit(solution)/shard_map/ppermute | solution.py:342
  15.4 2.7 %collective-permute-done.6.refs_0_.refs_10_ = bf16[16,4608]{1,0:T(8,128)(2,1)S(1)} collective-permute-done((bf16[16,4608]{1,0:T(8,128)(2,1)S(1)}, bf16[16,4608]{1,0:T(8,128)(2,1)S(1)}, u32[]{:S(2)}, u32[]{:S(2)}) %collective-permute-start.6) | collective-permute-done | bytes 147488 | tf_op jit(solution)/shard_map/ppermute | solution.py:342
  18.1 1.5 %collective-permute-start.5 = (bf16[16,4608]{1,0:T(8,128)(2,1)S(1)}, bf16[16,4608]{1,0:T(8,128)(2,1)S(1)}, u32[]{:S(2)}, u32[]{:S(2)}) collective-permute-start(bf16[16,4608]{1,0:T(8,128)(2,1)S(1)} %collective-permute-done.4.refs_2_.refs_8_), channel_id=1, source_target_pairs={{0,2},{1,3},{2,0},{3,1},{4,6},{5,7},{6,4},{7,5},{8,10},{9,11},{10,... | collective-permute-start | bytes 442376 | tf_op jit(solution)/shard_map/ppermute | solution.py:342
  19.6 0.4 collective-permute-start.8
  20.0 0.5 collective-permute-start.7
  20.5 1.5 %collective-permute-start.3 = (bf16[16,4608]{1,0:T(8,128)(2,1)S(1)}, bf16[16,4608]{1,0:T(8,128)(2,1)S(1)}, u32[]{:S(2)}, u32[]{:S(2)}) collective-permute-start(bf16[16,4608]{1,0:T(8,128)(2,1)S(1)} %maximum_maximum_fusion.refs_0_.refs_6_), channel_id=1, source_target_pairs={{0,2},{1,3},{2,0},{3,1},{4,6},{5,7},{6,4},{7,5},{8,10},{9,11},{10,... | collective-permute-start | bytes 442376 | tf_op jit(solution)/shard_map/ppermute | solution.py:342
  22.7 0.0 copy-done.11
  22.7 0.6 reshape.31.owner_ref
  23.3 1.5 %collective-permute-done.5.refs_3_.refs_9_ = bf16[16,4608]{1,0:T(8,128)(2,1)S(1)} collective-permute-done((bf16[16,4608]{1,0:T(8,128)(2,1)S(1)}, bf16[16,4608]{1,0:T(8,128)(2,1)S(1)}, u32[]{:S(2)}, u32[]{:S(2)}) %collective-permute-start.5) | collective-permute-done | bytes 147488 | tf_op jit(solution)/shard_map/ppermute | solution.py:342
  24.8 0.0 collective-permute-done.8.refs_5_.refs_12_
  24.8 1.6 %collective-permute-start.9 = (bf16[16,4608]{1,0:T(8,128)(2,1)S(1)}, bf16[16,4608]{1,0:T(8,128)(2,1)S(1)}, u32[]{:S(2)}, u32[]{:S(2)}) collective-permute-start(bf16[16,4608]{1,0:T(8,128)(2,1)S(1)} %collective-permute-done.8.refs_5_.refs_12_), channel_id=1, source_target_pairs={{0,2},{1,3},{2,0},{3,1},{4,6},{5,7},{6,4},{7,5},{8,10},{9,11},{10,... | collective-permute-start | bytes 442376 | tf_op jit(solution)/shard_map/ppermute | solution.py:342
  26.4 1.5 %collective-permute-done.7.refs_1_.refs_11_ = bf16[16,4608]{1,0:T(8,128)(2,1)S(1)} collective-permute-done((bf16[16,4608]{1,0:T(8,128)(2,1)S(1)}, bf16[16,4608]{1,0:T(8,128)(2,1)S(1)}, u32[]{:S(2)}, u32[]{:S(2)}) %collective-permute-start.7) | collective-permute-done | bytes 147488 | tf_op jit(solution)/shard_map/ppermute | solution.py:342
  27.9 0.0 collective-permute-done.2.refs_5_.refs_3_.refs_2_
  28.0 10.0 %early_stats.3.refs_4_ = f32[2,4,128]{2,1,0:T(4,128)S(1)} custom-call(bf16[16,4608]{1,0:T(8,128)(2,1)S(1)} %collective-permute-done.6.refs_0_.refs_10_, bf16[16,4608]{1,0:T(8,128)(2,1)S(1)} %collective-permute-done.7.refs_1_.refs_11_, bf16[1024,512]{1,0:T(8,128)(2,1)S(1)} %get-tuple-element.24.refs_4_.refs_2_.refs_1_, ...), custom_call_target="tpu_custom_call" | custom-call | flops 536870912 | bytes 1048576 | tf_op jit(solution)/shard_map/early_stats/pallas_call | solution.py:391
  38.0 0.0 collective-permute-done.3.refs_1_.refs_7_
  38.0 13.6 %early_stats.2.refs_3_ = f32[4,4,128]{2,1,0:T(4,128)S(1)} custom-call(bf16[16,4608]{1,0:T(8,128)(2,1)S(1)} %maximum_maximum_fusion.refs_0_.refs_6_, bf16[16,4608]{1,0:T(8,128)(2,1)S(1)} %collective-permute-done.3.refs_1_.refs_7_, bf16[16,4608]{1,0:T(8,128)(2,1)S(1)} %collective-permute-done.4.refs_2_.refs_8_, ...), custom_call_target="tpu_custom_call" | custom-call | flops 1073741824 | bytes 1048576 | tf_op jit(solution)/shard_map/early_stats/pallas_call | solution.py:391
  51.6 0.0 copy-start.12
  51.7 0.0 collective-permute-done.9.refs_6_.refs_13_
  51.7 2.1 %late_stats.1 = f32[8,8,4,128]{3,2,1,0:T(4,128)} custom-call(s32[1]{0:T(128)} %bitcast.refs_0_, bf16[1024,512]{1,0:T(8,128)(2,1)S(1)} %get-tuple-element.24.refs_4_.refs_2_.refs_1_, bf16[1024,512]{1,0:T(8,128)(2,1)S(1)} %collective-permute-done.2.refs_5_.refs_3_.refs_2_, f32[4,4,128]{2,1,0:T(4,128)S(1)} %early_stats.2.refs_3_, ...), custom_call_target="tpu_custom_call" | custom-call | flops 536870912 | bytes 1048576 | tf_op jit(solution)/shard_map/late_stats/pallas_call | solution.py:441
  53.8 11.3 %all-to-all-start = ((f32[8,8,4,128]{3,2,1,0:T(4,128)}), f32[8,8,4,128]{3,2,1,0:T(4,128)S(1)}, u32[]{:S(2)}, u32[]{:S(2)}) async-start(f32[8,8,4,128]{3,2,1,0:T(4,128)} %late_stats.1), calls=%async_computation | async-start | bytes 262144 | tf_op jit(solution)/shard_map/all_to_all | solution.py:484
  65.1 0.6 reshape.30.entry_ref
  65.7 6.4 %compact.1 = (bf16[640,256]{1,0:T(8,128)(2,1)}, f32[8,640]{1,0:T(8,128)}) custom-call(s32[1]{0:T(128)S(6)} %copy.10.count_ref, s32[1,640]{1,0:T(1,128)} %reshape.30.entry_ref, s32[1,640]{1,0:T(1,128)} %reshape.31.owner_ref, bf16[1024,1024]{1,0:T(8,128)(2,1)} %k_source.1, bf16[1024,1024]{1,0:T(8,128)(2,1)} %v_source.1), custom_call_target="tpu_custom_call" | custom-call | flops 2684354560 | bytes 4194304 | tf_op jit(solution)/shard_map/compact/pallas_call | solution.py:452
  72.1 0.4 all-to-all-done.refs_1_
  72.5 5.8 %all-to-all-start.1 = ((bf16[16,40,256]{2,1,0:T(8,128)(2,1)}), bf16[16,40,256]{2,1,0:T(8,128)(2,1)S(1)}, u32[]{:S(2)}, u32[]{:S(2)}) async-start(bf16[16,40,256]{2,1,0:T(8,128)(2,1)} %bitcast.5), calls=%async_computation.1 | async-start | bytes 655360 | tf_op jit(solution)/shard_map/all_to_all | solution.py:480
  78.2 0.4 collective-permute-start.10
  78.7 1.1 %collective-permute-done.10.refs_5_ = f32[8,640]{1,0:T(8,128)S(1)} collective-permute-done((f32[8,640]{1,0:T(8,128)}, f32[8,640]{1,0:T(8,128)S(1)}, u32[]{:S(2)}, u32[]{:S(2)}) %collective-permute-start.10) | collective-permute-done | bytes 20512 | tf_op jit(solution)/shard_map/ppermute | solution.py:342
  79.7 0.6 copy-done.13
  80.3 10.8 %mass.1 = (f32[4,1024]{1,0:T(4,128)}, f32[4,1024]{1,0:T(4,128)}, f32[16,2,128]{2,1,0:T(2,128)}) custom-call(s32[1]{0:T(128)} %bitcast.refs_0_, f32[8,8,4,128]{3,2,1,0:T(4,128)} %copy-done.10, bf16[1024,512]{1,0:T(8,128)(2,1)} %copy-done, bf16[1024,512]{1,0:T(8,128)(2,1)} %copy-done.1, f32[8,640]{1,0:T(8,128)} %get-tuple-element.17.refs_4_, ...), custom_call_target="tpu_custom_call" | custom-call | flops 2147483648 | bytes 1048576 | tf_op jit(solution)/shard_map/mass/pallas_call | solution.py:493
  91.1 0.4 collective-permute-start.11
  91.5 0.0 all-to-all-done.1
  91.5 5.8 %all-to-all-start.2 = ((f32[16,2,128]{2,1,0:T(2,128)}), f32[16,2,128]{2,1,0:T(2,128)S(1)}, u32[]{:S(2)}, u32[]{:S(2)}) async-start(f32[16,2,128]{2,1,0:T(2,128)} %get-tuple-element.22), calls=%async_computation.2 | async-start | bytes 32768 | tf_op jit(solution)/shard_map/all_to_all | solution.py:517
  97.3 0.0 collective-permute-done.11
  97.3 1.4 %maximum_select_fusion = f32[8,1024]{1,0:T(8,128)} fusion(f32[4,1024]{1,0:T(4,128)S(1)} %collective-permute-done.11, f32[4,1024]{1,0:T(4,128)} %get-tuple-element.18, pred[]{:T(512)S(6)} %eq.8), kind=kLoop, calls=%fused_computation.1 | loop fusion | flops 24576 | bytes 65537 | tf_op jit(solution)/shard_map/jit(_where)/select_n | solution.py:521
  98.7 5.1 %all-to-all-done.2 = f32[16,2,128]{2,1,0:T(2,128)S(1)} async-done(((f32[16,2,128]{2,1,0:T(2,128)}), f32[16,2,128]{2,1,0:T(2,128)S(1)}, u32[]{:S(2)}, u32[]{:S(2)}) %all-to-all-start.2) | async-done | bytes 16416 | tf_op jit(solution)/shard_map/all_to_all | solution.py:517
  103.8 0.7 convert_element_type.8
  104.5 0.7 copy.11
  (28 shorter events, 0.1 us)
Async XLA Ops:
  1.4 1.4 %collective-permute-start.1 = (bf16[8,1024]{1,0:T(8,128)(2,1)S(1)}, bf16[8,1024]{1,0:T(8,128)(2,1)S(1)}, u32[]{:S(2)}, u32[]{:S(2)}) collective-permute-start(bf16[8,1024]{1,0:T(8,128)(2,1)S(1)} %slice_select_fusion), channel_id=1, source_target_pairs={{0,1},{1,0},{2,3},{3,2},{4,5},{5,4},{6,7},{7,6},{8,9},{9,8},{10,11... | collective-permute-start | bytes 49160 | tf_op jit(solution)/shard_map/ppermute | solution.py:342
  1.8 1.6 %collective-permute-start = (bf16[8,8192]{1,0:T(8,128)(2,1)}, bf16[8,8192]{1,0:T(8,128)(2,1)S(1)}, u32[]{:S(2)}, u32[]{:S(2)}) collective-permute-start(bf16[8,8192]{1,0:T(8,128)(2,1)} %param.8), channel_id=1, source_target_pairs={{0,1},{1,0},{2,3},{3,2},{4,5},{5,4},{6,7},{7,6},{8,9},{9,8},{10,11... | collective-permute-start | bytes 393224 | tf_op jit(solution)/shard_map/ppermute | solution.py:342
  3.4 34.6 %copy-start.6 = (bf16[16,4608]{1,0:T(8,128)(2,1)}, bf16[16,4608]{1,0:T(8,128)(2,1)S(1)}, u32[]{:S(2)}) copy-start(bf16[16,4608]{1,0:T(8,128)(2,1)S(1)} %maximum_maximum_fusion.refs_0_.refs_6_) | copy-start | bytes 442372
  3.4 19.3 %copy-start.11 = (s32[640]{0:T(1024)S(1)}, s32[640]{0:T(1024)}, u32[]{:S(2)}) copy-start(s32[640]{0:T(1024)} %param.11) | copy-start | bytes 7684
  5.2 46.5 %copy-start = (bf16[1024,512]{1,0:T(8,128)(2,1)}, bf16[1024,512]{1,0:T(8,128)(2,1)S(1)}, u32[]{:S(2)}) copy-start(bf16[1024,512]{1,0:T(8,128)(2,1)S(1)} %get-tuple-element.24.refs_4_.refs_2_.refs_1_) | copy-start | bytes 3145732
  5.2 22.8 %collective-permute-start.2 = (bf16[1024,512]{1,0:T(8,128)(2,1)S(1)}, bf16[1024,512]{1,0:T(8,128)(2,1)S(1)}, u32[]{:S(2)}, u32[]{:S(2)}) collective-permute-start(bf16[1024,512]{1,0:T(8,128)(2,1)S(1)} %get-tuple-element.23), channel_id=1, source_target_pairs={{0,1},{1,0},{2,3},{3,2},{4,5},{5,4},{6,7},{7,6},{8,9},{9,8},{10,11... | collective-permute-start | bytes 3145736 | tf_op jit(solution)/shard_map/ppermute | solution.py:342
  5.4 10.0 %collective-permute-start.4 = (bf16[16,4608]{1,0:T(8,128)(2,1)S(1)}, bf16[16,4608]{1,0:T(8,128)(2,1)S(1)}, u32[]{:S(2)}, u32[]{:S(2)}) collective-permute-start(bf16[16,4608]{1,0:T(8,128)(2,1)S(1)} %maximum_maximum_fusion.refs_0_.refs_6_), channel_id=1, source_target_pairs={{0,4},{1,5},{2,6},{3,7},{4,0},{5,1},{6,2},{7,3},{8,12},{9,13},{10,... | collective-permute-start | bytes 442376 | tf_op jit(solution)/shard_map/ppermute | solution.py:342
  8.3 9.7 %collective-permute-start.6 = (bf16[16,4608]{1,0:T(8,128)(2,1)S(1)}, bf16[16,4608]{1,0:T(8,128)(2,1)S(1)}, u32[]{:S(2)}, u32[]{:S(2)}) collective-permute-start(bf16[16,4608]{1,0:T(8,128)(2,1)S(1)} %maximum_maximum_fusion.refs_0_.refs_6_), channel_id=1, source_target_pairs={{0,8},{1,9},{2,10},{3,11},{4,12},{5,13},{6,14},{7,15},{8,0},{9,1},... | collective-permute-start | bytes 442376 | tf_op jit(solution)/shard_map/ppermute | solution.py:342
  15.4 36.2 %copy-start.7 = (bf16[16,4608]{1,0:T(8,128)(2,1)}, bf16[16,4608]{1,0:T(8,128)(2,1)S(1)}, u32[]{:S(2)}) copy-start(bf16[16,4608]{1,0:T(8,128)(2,1)S(1)} %collective-permute-done.4.refs_2_.refs_8_) | copy-start | bytes 442372
  18.1 33.6 %copy-start.2 = (bf16[16,4608]{1,0:T(8,128)(2,1)}, bf16[16,4608]{1,0:T(8,128)(2,1)S(1)}, u32[]{:S(2)}) copy-start(bf16[16,4608]{1,0:T(8,128)(2,1)S(1)} %collective-permute-done.6.refs_0_.refs_10_) | copy-start | bytes 442372
  18.1 6.7 %collective-permute-start.5 = (bf16[16,4608]{1,0:T(8,128)(2,1)S(1)}, bf16[16,4608]{1,0:T(8,128)(2,1)S(1)}, u32[]{:S(2)}, u32[]{:S(2)}) collective-permute-start(bf16[16,4608]{1,0:T(8,128)(2,1)S(1)} %collective-permute-done.4.refs_2_.refs_8_), channel_id=1, source_target_pairs={{0,2},{1,3},{2,0},{3,1},{4,6},{5,7},{6,4},{7,5},{8,10},{9,11},{10,... | collective-permute-start | bytes 442376 | tf_op jit(solution)/shard_map/ppermute | solution.py:342
  19.6 5.2 %collective-permute-start.8 = (bf16[16,4608]{1,0:T(8,128)(2,1)S(1)}, bf16[16,4608]{1,0:T(8,128)(2,1)S(1)}, u32[]{:S(2)}, u32[]{:S(2)}) collective-permute-start(bf16[16,4608]{1,0:T(8,128)(2,1)S(1)} %collective-permute-done.6.refs_0_.refs_10_), channel_id=1, source_target_pairs={{0,4},{1,5},{2,6},{3,7},{4,0},{5,1},{6,2},{7,3},{8,12},{9,13},{10,... | collective-permute-start | bytes 442376 | tf_op jit(solution)/shard_map/ppermute | solution.py:342
  20.0 7.9 %collective-permute-start.7 = (bf16[16,4608]{1,0:T(8,128)(2,1)S(1)}, bf16[16,4608]{1,0:T(8,128)(2,1)S(1)}, u32[]{:S(2)}, u32[]{:S(2)}) collective-permute-start(bf16[16,4608]{1,0:T(8,128)(2,1)S(1)} %collective-permute-done.6.refs_0_.refs_10_), channel_id=1, source_target_pairs={{0,2},{1,3},{2,0},{3,1},{4,6},{5,7},{6,4},{7,5},{8,10},{9,11},{10,... | collective-permute-start | bytes 442376 | tf_op jit(solution)/shard_map/ppermute | solution.py:342
  20.5 17.4 %collective-permute-start.3 = (bf16[16,4608]{1,0:T(8,128)(2,1)S(1)}, bf16[16,4608]{1,0:T(8,128)(2,1)S(1)}, u32[]{:S(2)}, u32[]{:S(2)}) collective-permute-start(bf16[16,4608]{1,0:T(8,128)(2,1)S(1)} %maximum_maximum_fusion.refs_0_.refs_6_), channel_id=1, source_target_pairs={{0,2},{1,3},{2,0},{3,1},{4,6},{5,7},{6,4},{7,5},{8,10},{9,11},{10,... | collective-permute-start | bytes 442376 | tf_op jit(solution)/shard_map/ppermute | solution.py:342
  24.8 26.8 %copy-start.8 = (bf16[16,4608]{1,0:T(8,128)(2,1)}, bf16[16,4608]{1,0:T(8,128)(2,1)S(1)}, u32[]{:S(2)}) copy-start(bf16[16,4608]{1,0:T(8,128)(2,1)S(1)} %collective-permute-done.5.refs_3_.refs_9_) | copy-start | bytes 442372
  24.8 26.9 %copy-start.3 = (bf16[16,4608]{1,0:T(8,128)(2,1)}, bf16[16,4608]{1,0:T(8,128)(2,1)S(1)}, u32[]{:S(2)}) copy-start(bf16[16,4608]{1,0:T(8,128)(2,1)S(1)} %collective-permute-done.8.refs_5_.refs_12_) | copy-start | bytes 442372
  24.8 26.9 %collective-permute-start.9 = (bf16[16,4608]{1,0:T(8,128)(2,1)S(1)}, bf16[16,4608]{1,0:T(8,128)(2,1)S(1)}, u32[]{:S(2)}, u32[]{:S(2)}) collective-permute-start(bf16[16,4608]{1,0:T(8,128)(2,1)S(1)} %collective-permute-done.8.refs_5_.refs_12_), channel_id=1, source_target_pairs={{0,2},{1,3},{2,0},{3,1},{4,6},{5,7},{6,4},{7,5},{8,10},{9,11},{10,... | collective-permute-start | bytes 442376 | tf_op jit(solution)/shard_map/ppermute | solution.py:342
  27.9 23.7 %copy-start.4 = (bf16[16,4608]{1,0:T(8,128)(2,1)}, bf16[16,4608]{1,0:T(8,128)(2,1)S(1)}, u32[]{:S(2)}) copy-start(bf16[16,4608]{1,0:T(8,128)(2,1)S(1)} %collective-permute-done.7.refs_1_.refs_11_) | copy-start | bytes 442372
  28.0 23.7 %copy-start.1 = (bf16[1024,512]{1,0:T(8,128)(2,1)}, bf16[1024,512]{1,0:T(8,128)(2,1)S(1)}, u32[]{:S(2)}) copy-start(bf16[1024,512]{1,0:T(8,128)(2,1)S(1)} %collective-permute-done.2.refs_5_.refs_3_.refs_2_) | copy-start | bytes 3145732
  38.0 15.8 %copy-start.9 = (bf16[16,4608]{1,0:T(8,128)(2,1)}, bf16[16,4608]{1,0:T(8,128)(2,1)S(1)}, u32[]{:S(2)}) copy-start(bf16[16,4608]{1,0:T(8,128)(2,1)S(1)} %collective-permute-done.3.refs_1_.refs_7_) | copy-start | bytes 442372
  51.6 13.5 %copy-start.12 = (s32[640]{0:T(1024)S(1)}, s32[640]{0:T(1024)}, u32[]{:S(2)}) copy-start(s32[640]{0:T(1024)} %param.10) | copy-start | bytes 7684
  51.7 20.4 %copy-start.5 = (bf16[16,4608]{1,0:T(8,128)(2,1)}, bf16[16,4608]{1,0:T(8,128)(2,1)S(1)}, u32[]{:S(2)}) copy-start(bf16[16,4608]{1,0:T(8,128)(2,1)S(1)} %collective-permute-done.9.refs_6_.refs_13_) | copy-start | bytes 442372
  53.8 18.7 %all-to-all-start = ((f32[8,8,4,128]{3,2,1,0:T(4,128)}), f32[8,8,4,128]{3,2,1,0:T(4,128)S(1)}, u32[]{:S(2)}, u32[]{:S(2)}) async-start(f32[8,8,4,128]{3,2,1,0:T(4,128)} %late_stats.1), calls=%async_computation | async-start | bytes 262144 | tf_op jit(solution)/shard_map/all_to_all | solution.py:484
  72.5 7.2 %copy-start.10 = (f32[8,8,4,128]{3,2,1,0:T(4,128)}, f32[8,8,4,128]{3,2,1,0:T(4,128)S(1)}, u32[]{:S(2)}) copy-start(f32[8,8,4,128]{3,2,1,0:T(4,128)S(1)} %all-to-all-done.refs_1_) | copy-start | bytes 393220
  72.5 19.0 %all-to-all-start.1 = ((bf16[16,40,256]{2,1,0:T(8,128)(2,1)}), bf16[16,40,256]{2,1,0:T(8,128)(2,1)S(1)}, u32[]{:S(2)}, u32[]{:S(2)}) async-start(bf16[16,40,256]{2,1,0:T(8,128)(2,1)} %bitcast.5), calls=%async_computation.1 | async-start | bytes 655360 | tf_op jit(solution)/shard_map/all_to_all | solution.py:480
  78.2 1.5 %collective-permute-start.10 = (f32[8,640]{1,0:T(8,128)}, f32[8,640]{1,0:T(8,128)S(1)}, u32[]{:S(2)}, u32[]{:S(2)}) collective-permute-start(f32[8,640]{1,0:T(8,128)} %get-tuple-element.17.refs_4_), channel_id=1, source_target_pairs={{0,1},{1,0},{2,3},{3,2},{4,5},{5,4},{6,7},{7,6},{8,9},{9,8},{10,11... | collective-permute-start | bytes 61448 | tf_op jit(solution)/shard_map/ppermute | solution.py:342
  79.7 0.6 copy-start.13
  91.1 6.2 %collective-permute-start.11 = (f32[4,1024]{1,0:T(4,128)}, f32[4,1024]{1,0:T(4,128)S(1)}, u32[]{:S(2)}, u32[]{:S(2)}) collective-permute-start(f32[4,1024]{1,0:T(4,128)} %get-tuple-element.19), channel_id=1, source_target_pairs={{0,1},{1,0},{2,3},{3,2},{4,5},{5,4},{6,7},{7,6},{8,9},{9,8},{10,11... | collective-permute-start | bytes 49160 | tf_op jit(solution)/shard_map/ppermute | solution.py:342
  91.5 12.3 %all-to-all-start.2 = ((f32[16,2,128]{2,1,0:T(2,128)}), f32[16,2,128]{2,1,0:T(2,128)S(1)}, u32[]{:S(2)}, u32[]{:S(2)}) async-start(f32[16,2,128]{2,1,0:T(2,128)} %get-tuple-element.22), calls=%async_computation.2 | async-start | bytes 32768 | tf_op jit(solution)/shard_map/all_to_all | solution.py:517

commit v3 on v2

--- a/solution.py
+++ b/solution.py
@@ -38,9 +38,35 @@
     return lax.broadcasted_iota(jnp.int32, shape, dim)
 
 
-def compact_kernel(
-    peers, count_ref, entry_ref, owner_ref, k_source, v_source, rows_ref, code_ref, k_ref, v_ref, sems
-):
+def codes_kernel(positions, peers, own_ref, sib_ref, own_code_ref, sib_code_ref, column_ref):
+    for mine, ref, code_ref in ((True, own_ref, own_code_ref), (False, sib_ref, sib_code_ref)):
+        slots = ref.shape[1]
+        entry, owner, count = ref[0:1], ref[1:2], ref[2:3]
+        capacity = slots // peers
+        live = iota((1, slots), 1) < count
+        member = jnp.where((owner == iota((peers, slots), 0)) & live, 1.0, 0.0)
+        before = one_hot(iota((slots, slots), 0) < iota((slots, slots), 1))
+        earlier = jnp.dot(member.astype(jnp.bfloat16), before, preferred_element_type=jnp.float32)
+        rank = jnp.sum(earlier * member, axis=0, keepdims=True).astype(jnp.int32)
+        target = jnp.where(live, owner * capacity + rank, -1)
+        placed = one_hot(iota((slots, slots), 0) == target)
+        token, head = entry % positions, entry // positions
+        line = iota((8, slots), 0)
+        facts = jnp.where(
+            line == 0, 1, jnp.where(line == 1, head, jnp.where(line == 2, token // 64, token % 64))
+        )
+        facts = facts.astype(jnp.float32).astype(jnp.bfloat16)
+        by_row = nt(facts, placed)
+        row_token = jnp.where(by_row[0:1] > 0.5, by_row[2:3] * 64 + by_row[3:4], -1.0)
+        code_ref[...] = jnp.where(line == 0, row_token, by_row[1:2])
+        if mine:
+            by_col = nt(placed, facts)
+            col_token = jnp.where(by_col[:, 0:1] > 0.5, by_col[:, 2:3] * 64 + by_col[:, 3:4], -1.0)
+            column = jnp.where(iota((slots, 8), 1) == 0, col_token, by_col[:, 1:2])
+            column_ref[...] = column
+
+
+def compact_kernel(column_ref, k_source, v_source, packed_ref, k_ref, v_ref, rows_ref, sems):
     copies = (
         pltpu.make_async_copy(k_source, k_ref, sems.at[0]),
         pltpu.make_async_copy(v_source, v_ref, sems.at[1]),
@@ -48,44 +74,25 @@
     for copy in copies:
         copy.start()
     positions = k_ref.shape[0]
-    slots = entry_ref.shape[1]
-    capacity = slots // peers
-    owner, entry = owner_ref[...], entry_ref[...]
-    live = iota((1, slots), 1) < count_ref[0]
-    member = jnp.where((owner == iota((peers, slots), 0)) & live, 1.0, 0.0)
-    before = one_hot(iota((slots, slots), 0) < iota((slots, slots), 1))
-    earlier = jnp.dot(member.astype(jnp.bfloat16), before, preferred_element_type=jnp.float32)
-    rank = jnp.sum(earlier * member, axis=0, keepdims=True).astype(jnp.int32)
-    target = jnp.where(live, owner * capacity + rank, -1)
-    placed = one_hot(iota((slots, slots), 0) == target)
-    token, head = entry % positions, entry // positions
-    line = iota((8, slots), 0)
-    facts = jnp.where(
-        line == 0, 1, jnp.where(line == 1, head, jnp.where(line == 2, token // 64, token % 64))
-    )
-    facts = facts.astype(jnp.float32).astype(jnp.bfloat16)
-    by_row = nt(facts, placed)
-    row_token = jnp.where(by_row[0:1] > 0.5, by_row[2:3] * 64 + by_row[3:4], -1.0)
-    code_ref[...] = jnp.where(iota((8, slots), 0) == 0, row_token, by_row[1:2])
-    by_col = nt(placed, facts)
-    col_head = by_col[:, 1:2].astype(jnp.int32)
-    col_token = jnp.where(by_col[:, 0:1] > 0.5, by_col[:, 2:3] * 64 + by_col[:, 3:4], -1.0)
-    col_token = col_token.astype(jnp.int32)
-    step = 128 if slots % 128 == 0 else slots
+    slots = rows_ref.shape[0]
+    token = column_ref[:, 0:1].astype(jnp.int32)
+    head = column_ref[:, 1:2].astype(jnp.int32)
+    pick = one_hot(iota((slots, positions), 1) == token)
     for side, source in enumerate((k_ref, v_ref)):
         copies[side].wait()
-        for start in range(0, slots, step):
-            token_part = col_token[start : start + step]
-            head_part = col_head[start : start + step]
-            pick = one_hot(iota((step, positions), 1) == token_part)
-            found = jnp.dot(pick, source[...], preferred_element_type=jnp.float32)
-            kept = jnp.zeros((step, HEAD_DIM), jnp.float32)
-            for g in range(KV_HEADS):
-                part = found[:, g * HEAD_DIM : (g + 1) * HEAD_DIM]
-                kept = kept + jnp.where(head_part == g, part, 0.0)
-            rows_ref[start : start + step, side * HEAD_DIM : (side + 1) * HEAD_DIM] = kept.astype(
-                jnp.bfloat16
-            )
+        kept = jnp.zeros((slots, HEAD_DIM), jnp.float32)
+        for g in range(0, KV_HEADS, 2):
+            pair = source[:, g * HEAD_DIM : (g + 2) * HEAD_DIM]
+            found = jnp.dot(pick, pair, preferred_element_type=jnp.float32)
+            kept = kept + jnp.where(head == g, found[:, :HEAD_DIM], 0.0)
+            kept = kept + jnp.where(head == g + 1, found[:, HEAD_DIM:], 0.0)
+        rows_ref[:, side * HEAD_DIM : (side + 1) * HEAD_DIM] = kept
+    peers, room, width = packed_ref.shape
+    capacity = slots // peers
+    rest = jnp.zeros((room - capacity, width), jnp.float32)
+    for p in range(peers):
+        rows = rows_ref[p * capacity : (p + 1) * capacity, :]
+        packed_ref[p] = jnp.concatenate([rows, rest], axis=0).astype(jnp.bfloat16)
 
 
 def query_rows(block_refs, g):
@@ -100,22 +107,6 @@
 def spread(limits, value):
     low, high = limits
     return jnp.minimum(low, jnp.min(value)), jnp.maximum(high, jnp.max(value))
-
-
-def fetch_keys(sources, held, sems):
-    copies = []
-    for g in range(HALF):
-        for i, source in enumerate(sources):
-            cols = slice(g * HEAD_DIM, (g + 1) * HEAD_DIM)
-            copies.append(pltpu.make_async_copy(source.at[:, cols], held.at[g, i], sems.at[g, i]))
-    for copy in copies:
-        copy.start()
-
-    def wait(g):
-        for copy in copies[2 * g : 2 * g + 2]:
-            copy.wait()
-
-    return wait
 
 
 def local_stats(block_refs, k_refs, store):
@@ -171,13 +162,6 @@
     return 0 if offset is None else chip ^ offset
 
 
-def fetch(sources, held, sems):
-    copies = [pltpu.make_async_copy(x, held.at[i], sems.at[i]) for i, x in enumerate(sources)]
-    for copy in copies:
-        copy.start()
-    return copies
-
-
 def early_stats_kernel(count, *refs):
     blocks, k_refs, out_ref = refs[:count], refs[count : count + 2], refs[-1]
 
@@ -206,13 +190,6 @@
         out_ref[d] = everything
 
 
-def fetch(sources, held, sems):
-    copies = [pltpu.make_async_copy(x, held.at[i], sems.at[i]) for i, x in enumerate(sources)]
-    for copy in copies:
-        copy.start()
-    return copies
-
-
 def split3(x):
     high = x.astype(jnp.bfloat16)
     rest = x - high.astype(jnp.float32)
@@ -221,19 +198,16 @@
     return high, middle, low
 
 
-def mass_kernel(offsets, peers, factor, width, edges, *refs):
+def mass_kernel(offsets, peers, factor, width, edges, score_row, *refs):
     count = len(offsets)
     place_ref, stats_ref, k_own, k_sib = refs[:4]
-    code_sources = refs[4:6]
-    edge_refs, refs = refs[6 : 6 + edges], refs[6 + edges :]
-    sources = refs[:count]
-    imp_own, imp_sib, score_ref = refs[count : count + 3]
-    lse_ref, side_ref, blocks_held, held, codes, block_sems, sems, code_sems = refs[count + 3 :]
-    copies = fetch(sources, blocks_held, block_sems)
-    wait = fetch_keys((k_own, k_sib), held, sems)
-    code_copies = fetch(code_sources, codes, code_sems)
-    blocks = [blocks_held.at[i] for i in range(count)]
-    tokens = held.shape[2]
+    codes, packed_ref = refs[4:6], refs[6]
+    edge_refs, refs = refs[7 : 7 + edges], refs[7 + edges :]
+    blocks = refs[:count]
+    imp_own, imp_sib, out_ref, lse_ref, side_ref, sem = refs[count:]
+    copy = pltpu.make_async_copy(packed_ref, out_ref, sem)
+    copy.start()
+    tokens = k_own.shape[0]
     core = place_ref[0] % 2
     chip = place_ref[0] // 2
     chips = peers // 2
@@ -243,8 +217,6 @@
     top = jnp.max(stats, axis=0)
     lse_ref[...] = top + jnp.log2(jnp.sum(jnp.exp2(stats - top[None]), axis=0))
 
-    for copy in copies:
-        copy.wait()
     step = min(512, tokens)
     found = [[], []]
     rims = []
@@ -258,12 +230,12 @@
             parts, jnp.ones((8, HEAD_DIM), jnp.bfloat16), (((0,), (0,)), ((), ())),
             preferred_element_type=jnp.float32,
         )
-        wait(g)
-        for i in range(2):
+        cols = slice(g * HEAD_DIM, (g + 1) * HEAD_DIM)
+        for i, k_ref in enumerate((k_own, k_sib)):
             line = []
             for start in range(0, tokens, step):
                 shift = jnp.concatenate([side_ref[...]] * (step // HEAD_DIM), axis=1)
-                weights = jnp.exp2(nt(rows, held[g, i, start : start + step, :]) * SCALE2 - shift)
+                weights = jnp.exp2(nt(rows, k_ref[start : start + step, cols]) * SCALE2 - shift)
                 line.append(jnp.sum(weights, axis=0, keepdims=True))
             found[i].append(jnp.concatenate(line, axis=1))
         if edges:
@@ -274,8 +246,10 @@
             cols = slice(width + g * HEAD_DIM, width + (g + 1) * HEAD_DIM)
             rim_keys = []
             for other in (chip ^ jnp.maximum(chip - 1, 0), chip ^ jnp.minimum(chip + 1, chips - 1)):
-                where = sum(jnp.where(other == off, i, 0) for i, off in enumerate(offsets))
-                rim_keys.append(blocks_held[where, :, cols])
+                found_keys = blocks[0][:, cols]
+                for off, ref in zip(offsets[1:], blocks[1:]):
+                    found_keys = jnp.where(other == off, ref[:, cols], found_keys)
+                rim_keys.append(found_keys)
         weights = jnp.exp2(nt(jnp.concatenate(rim_keys, axis=0), rows) * SCALE2 - lse)
         folded = weights[:, 0:HEAD_DIM]
         for first in range(HEAD_DIM, weights.shape[1], HEAD_DIM):
@@ -292,7 +266,7 @@
         before = jnp.where(is_low, rim_own, rim_sib)[:, EDGE - side :]
         after = jnp.where(is_low, rim_sib, rim_own)[:, :side]
     else:
-        size = blocks_held.shape[1]
+        size = blocks[0].shape[0]
         mid = size // 2
         before = jnp.where(is_low, rim[:, size - side : size], rim[:, mid - side : mid])
         after = jnp.where(is_low, rim[:, size : size + side], rim[:, size + mid : size + mid + side])
@@ -306,20 +280,23 @@
     halves = (importance[:, :tokens], importance[:, tokens:])
     imp_own[...] = jnp.where(is_low, halves[0], halves[1])
     imp_sib[...] = jnp.where(is_low, halves[1], halves[0])
-    for copy in code_copies:
-        copy.wait()
-    slots = codes.shape[2]
+    slots = codes[0].shape[1]
     capacity = slots // peers
+    scores = []
     for side in range(2):
-        code = jnp.where(core == side, codes[0], codes[1]).astype(jnp.int32)
+        code = jnp.where(core == side, codes[0][...], codes[1][...]).astype(jnp.int32)
         parts = jnp.concatenate(split3(halves[side]), axis=0)
         pick = one_hot(iota((tokens, slots), 0) == code[0:1])
         hits = jnp.dot(parts, pick, preferred_element_type=jnp.float32)
         value = hits[0:HALF] + hits[HALF : 2 * HALF] + hits[2 * HALF : 3 * HALF]
         mine = iota((HALF, slots), 0) + core * HALF == code[1:2]
-        score = jnp.sum(jnp.where(mine, value, 0.0), axis=0, keepdims=True)
-        for p in range(peers):
-            score_ref[p, side : side + 1, 0:capacity] = score[:, p * capacity : (p + 1) * capacity]
+        scores.append(jnp.sum(jnp.where(mine, value, 0.0), axis=0, keepdims=True))
+    both = jnp.concatenate(scores + [jnp.zeros((6, slots), jnp.float32)], axis=0)
+    copy.wait()
+    for p in range(peers):
+        out_ref[p, score_row : score_row + 8, 0:capacity] = both[
+            :, p * capacity : (p + 1) * capacity
+        ].astype(jnp.bfloat16)
 
 
 def after(x, *earlier):
@@ -347,13 +324,19 @@
     def joined(parts):
         return jnp.concatenate(parts, axis=0)
 
+    sibling_queries = swap(window_queries, 1)
+    own_queries = half(window_queries, core, half_queries)
+    ready_keys = after(cached_keys, sibling_queries)
+    k_own = half(ready_keys, core, half_keys)
+    k_other = half(ready_keys, 1 - core, half_keys)
+    k_sib = swap(k_other, 1)
+
     lines = chips // 2
     shard_rows = window_queries.shape[0]
     stepwise = shard_rows % 8 == 0 and chips % 4 == 0 and lines & (lines - 1) == 0
     edge = shard_rows if stepwise else EDGE
     rim = jnp.where(core == 1, cached_keys[positions - edge :], cached_keys[:edge])
-    sibling_queries = swap(window_queries, 1)
-    pair = [half(window_queries, core, half_queries), half(sibling_queries, core, half_queries)]
+    pair = [own_queries, half(sibling_queries, core, half_queries)]
     if stepwise:
         sibling_rim = swap(rim, 1)
         ends = [half(rim, core, half_keys), half(sibling_rim, core, half_keys)]
@@ -366,18 +349,6 @@
         edge_own = lax.ppermute(rim, "seq", ring + [(b, a) for a, b in ring])
         edges = [edge_own, swap(edge_own, 1)]
 
-    def keys_held():
-        return [
-            pltpu.VMEM((HALF, 2, positions, HEAD_DIM), jnp.bfloat16),
-            pltpu.SemaphoreType.DMA((HALF, 2)),
-        ]
-
-    def blocks_held(some):
-        return [
-            pltpu.VMEM((len(some),) + some[0].shape, jnp.bfloat16),
-            pltpu.SemaphoreType.DMA((len(some),)),
-        ]
-
     def score_cost(some):
         queries = len(some) * HALF * GROUP * some[0].shape[0]
         return pl.CostEstimate(
@@ -400,6 +371,7 @@
 
     if stepwise:
         line, distance = [(0, piece)], lines // 2
+        beside = {0: swap(piece, 2)}
         while distance:
             for off, block in list(line):
                 if distance == 1 and off == 0:
@@ -407,30 +379,41 @@
                     line.append((2, near))
                 else:
                     if distance == 1:
-                        block = after(block, near)
+                        block = after(block, near, beside[0])
                     line.append((off ^ 2 * distance, swap(block, 4 * distance)))
             distance //= 2
-        beside = {off: swap(block, 2) for off, block in line[:-1]}
+        beside.update({off: swap(block, 2) for off, block in line[1:-1]})
         start = [(0, piece), (1, beside[0]), (2, near), (3, beside[2])]
         sets = [start]
         for off, block in line[:-1]:
             if off not in (0, 2):
                 sets.append([(off, block), (off ^ 1, beside[off])])
         final = line[-1]
-        ready_keys = after(cached_keys, piece)
+        arrived = (line[1][1], near, beside[0])
     else:
         same_core = [[i for i in range(peers) if i % 2 == c] for c in range(2)]
         gathered = lax.all_gather(piece, "seq", axis=0, tiled=True, axis_index_groups=same_core)
         sets, final = [], (None, gathered)
-        ready_keys = after(cached_keys, piece)
-
-    k_own = half(ready_keys, core, half_keys)
-    k_sib = swap(half(ready_keys, 1 - core, half_keys), 1)
+        arrived = piece
+
+    facts = jnp.stack([after(kept_entry, arrived), row_owner, jnp.broadcast_to(kept_count, (slots,))])
+    code_own, code_sib, code_column = pl.pallas_call(
+        functools.partial(codes_kernel, positions, peers),
+        out_shape=(
+            jax.ShapeDtypeStruct((8, slots), jnp.float32),
+            jax.ShapeDtypeStruct((8, slots), jnp.float32),
+            jax.ShapeDtypeStruct((slots, 8), jnp.float32),
+        ),
+        in_specs=[VMEM, VMEM],
+        out_specs=(VMEM, VMEM, VMEM),
+        compiler_params=pltpu.CompilerParams(vmem_limit_bytes=8 * MIB),
+        name="codes",
+    )(facts, swap(facts, 1))
 
     first = [early_stats([block for _, block in some]) for some in sets]
     if stepwise:
         off, block = final
-        sets.append([final, (off ^ 1, swap(after(block, beside[2]), 2))])
+        sets.append([final, (off ^ 1, swap(after(block, beside[2], code_own), 2))])
     else:
         sets.append([final])
     blocks = [block for some in sets for _, block in some]
@@ -449,17 +432,17 @@
         name="late_stats",
     )(place, k_own, k_sib, *first, *late)
 
-    rows_out, code_own = pl.pallas_call(
-        functools.partial(compact_kernel, peers),
-        out_shape=(
-            jax.ShapeDtypeStruct((slots, 2 * HEAD_DIM), jnp.bfloat16),
-            jax.ShapeDtypeStruct((8, slots), jnp.float32),
-        ),
-        in_specs=[SMEM, VMEM, VMEM, ANYWHERE, ANYWHERE],
-        out_specs=(VMEM, VMEM),
+    score_row = -(-capacity // 8) * 8
+    room = -(-(score_row + 8) // 16) * 16
+    packed = pl.pallas_call(
+        compact_kernel,
+        out_shape=jax.ShapeDtypeStruct((peers, room, 2 * HEAD_DIM), jnp.bfloat16),
+        in_specs=[VMEM, ANYWHERE, ANYWHERE],
+        out_specs=VMEM,
         scratch_shapes=[
             pltpu.VMEM(cached_keys.shape, jnp.bfloat16),
             pltpu.VMEM(cached_values.shape, jnp.bfloat16),
+            pltpu.VMEM((slots, 2 * HEAD_DIM), jnp.float32),
             pltpu.SemaphoreType.DMA((2,)),
         ],
         compiler_params=pltpu.CompilerParams(vmem_limit_bytes=GRANT),
@@ -469,18 +452,7 @@
             transcendentals=0,
         ),
         name="compact",
-    )(
-        kept_count,
-        after(kept_entry, sent).reshape(1, slots),
-        row_owner.reshape(1, slots),
-        cached_keys,
-        cached_values,
-    )
-    code_sib = swap(code_own, 1)
-    got_rows = lax.all_to_all(
-        rows_out.reshape(peers, capacity, 2 * HEAD_DIM), "seq", split_axis=0, concat_axis=0, tiled=True
-    ).reshape(slots, 2 * HEAD_DIM)
-
+    )(after(code_column, sent), cached_keys, cached_values)
     stats = lax.all_to_all(
         sent,
         "seq",
@@ -490,33 +462,29 @@
         axis_index_groups=[[i for i in range(peers) if i % 2 == c] for c in range(2)],
     )
     factor = peers * positions / (GROUP * WINDOW * POOL)
-    imp_own, imp_sib, score = pl.pallas_call(
-        functools.partial(mass_kernel, offsets, peers, factor, half_queries, len(edges)),
+    imp_own, imp_sib, sending = pl.pallas_call(
+        functools.partial(mass_kernel, offsets, peers, factor, half_queries, len(edges), score_row),
         out_shape=(
             jax.ShapeDtypeStruct((HALF, positions), jnp.float32),
             jax.ShapeDtypeStruct((HALF, positions), jnp.float32),
-            jax.ShapeDtypeStruct((peers, 2, 128), jnp.float32),
+            jax.ShapeDtypeStruct(packed.shape, packed.dtype),
         ),
-        in_specs=[SMEM, VMEM] + [ANYWHERE] * 4 + [VMEM] * len(edges) + [ANYWHERE] * count,
+        in_specs=[SMEM] + [VMEM] * 5 + [ANYWHERE] + [VMEM] * (len(edges) + count),
         out_specs=(VMEM, VMEM, VMEM),
         scratch_shapes=[
             pltpu.VMEM((count, HALF, per_block), jnp.float32),
             pltpu.VMEM((count * per_block, HEAD_DIM), jnp.float32),
-            blocks_held(blocks)[0],
-            keys_held()[0],
-            pltpu.VMEM((2, 8, slots), jnp.float32),
-            blocks_held(blocks)[1],
-            keys_held()[1],
-            pltpu.SemaphoreType.DMA((2,)),
+            pltpu.SemaphoreType.DMA,
         ],
-        compiler_params=pltpu.CompilerParams(vmem_limit_bytes=GRANT),
+        compiler_params=pltpu.CompilerParams(vmem_limit_bytes=12 * MIB),
         cost_estimate=score_cost(blocks),
         name="mass",
-    )(place, stats, k_own, k_sib, code_own, code_sib, *edges, *blocks)
-
-    got_score = lax.all_to_all(after(score, got_rows), "seq", split_axis=0, concat_axis=0, tiled=True)
-    by_core = got_score.reshape(chips, 2, 2, 128)[..., :capacity]
-    score_out = (by_core[:, 0] + by_core[:, 1]).astype(jnp.bfloat16)
+    )(place, stats, k_own, k_sib, code_own, code_sib, packed, *edges, *blocks)
+
+    got = lax.all_to_all(sending, "seq", split_axis=0, concat_axis=0, tiled=True)
+    by_core = got[:, score_row : score_row + 2, :capacity].reshape(chips, 2, 2, capacity)
+    score_out = by_core[:, 0] + by_core[:, 1]
+    got_rows = got[:, :capacity]
     imp_other = swap(imp_sib, 1)
     importance = jnp.where(
         core == 0,
@@ -525,7 +493,7 @@
     )
     return (
         importance,
-        got_rows,
+        got_rows.reshape(slots, 2 * HEAD_DIM),
         score_out.reshape(peers * capacity),
     )
 

time: 104 us -> 97 us (0.933)
  Pallas kernels: 42.9 us -> 29.4 us
  waiting for transfers between devices: 17.3 us -> 21.5 us
  starting transfers between devices: 35.5 us -> 38.1 us
    pallas_call x2, Pallas kernels: 23.6 us -> 12.5 us  [early_stats(): pl.pallas_call(functools.partial(early_stats_kernel, len(some)), out_shap...]
    all_to_all x2 -> x1, starting transfers between devices: 11.5 us -> 20.5 us  [per_device(): lax.all_to_all(sending, 'seq', split_axis=0, concat_axis=0, tiled=True)]
    all_to_all x2 -> x1, waiting for transfers between devices: 5.06 us -> 10.3 us  [per_device(): lax.all_to_all(sending, 'seq', split_axis=0, concat_axis=0, tiled=True)]
    all_to_all x1, starting transfers between devices: 11.3 us -> 6.29 us  [per_device(): lax.all_to_all(sent, 'seq', split_axis=0, concat_axis=0, tiled=True, axis...]
    pallas_call x1, Pallas kernels: 10.8 us -> 7.06 us  [per_device(): pl.pallas_call(functools.partial(mass_kernel, offsets, peers, factor, hal...]
    ppermute x12, waiting for transfers between devices: 11.8 us -> 10.3 us  [swap(): return lax.ppermute(x, 'seq', [(i, i ^ distance) for i in range(peers)])]
    ppermute x12, starting transfers between devices: 12.7 us -> 11.3 us  [swap(): return lax.ppermute(x, 'seq', [(i, i ^ distance) for i in range(peers)])]
    pallas_call x1 -> x2, Pallas kernels: 6.36 us -> 7.7 us  [the longest x1 6.4 us: per_device(): pl.pallas_call(compact_kernel, out_shape=jax.ShapeDtypeStruct((peers, roo...]
  transfers between devices with their start and end apart: 15 -> 14, of which waited for: 8 -> 9; matrix products, arithmetic and copies ran while one was open for 3% -> 2% of each run, Pallas kernels for 39% -> 21%
where the time goes in v3:
time: 97 us; the launch traced here: 97.7 us
  starting transfers between devices  38.1 us (39%)
  Pallas kernels  29.4 us (30%)
  waiting for transfers between devices  21.5 us (22%)
  local copies, waits for them, and re-layouts  5.79 us (6%)
  other arithmetic  1.46 us (2%)
  between operations  1.38 us (1%)
    all_to_all x1, starting transfers between devices, per_device(): lax.all_to_all(sending, 'seq', split_axis=0, concat_axis=0, tiled=True)  20.5 us
    pallas_call x2, Pallas kernels, early_stats(): pl.pallas_call(functools.partial(early_stats_kernel, len(some)), out_shap...  12.5 us
    ppermute x12, starting transfers between devices, swap(): return lax.ppermute(x, 'seq', [(i, i ^ distance) for i in range(peers)])  11.3 us
    all_to_all x1, waiting for transfers between devices, per_device(): lax.all_to_all(sending, 'seq', split_axis=0, concat_axis=0, tiled=True)  10.3 us
    ppermute x12, waiting for transfers between devices, swap(): return lax.ppermute(x, 'seq', [(i, i ^ distance) for i in range(peers)])  10.3 us
    pallas_call x1, Pallas kernels, per_device(): pl.pallas_call(functools.partial(mass_kernel, offsets, peers, factor, hal...  7.06 us
    pallas_call x1, Pallas kernels, per_device(): pl.pallas_call(compact_kernel, out_shape=jax.ShapeDtypeStruct((peers, roo...  6.4 us
    all_to_all x1, starting transfers between devices, per_device(): lax.all_to_all(sent, 'seq', split_axis=0, concat_axis=0, tiled=True, axis...  6.29 us
  transfers between devices with their start and end apart: 14, of which 9 were waited for; matrix products, arithmetic and copies ran while one was open for 2% of the time, Pallas kernels for 21%

profile of v3, /device:TPU:0, one launch (start us, length us, event | category | flops | bytes accessed | tf_op | source)
XLA Modules:
  0.0 97.7 jit_solution(13741874394173552030)
XLA Ops:
  0.6 0.5 collective-permute-start
  1.1 0.7 slice_select_fusion
  1.9 0.1 collective-permute-start.2
  1.9 0.8 constant_dynamic-slice_fusion.3
  2.8 0.3 collective-permute-done.2
  3.1 0.0 copy-start.2
  3.1 0.0 copy-start.3
  3.1 0.0 collective-permute-done
  3.1 1.7 %constant_dynamic-slice_fusion.4 = (bf16[1024,512]{1,0:T(8,128)(2,1)S(1)}, bf16[1024,512]{1,0:T(8,128)(2,1)S(1)}) fusion(bf16[1024,1024]{1,0:T(8,128)(2,1)} %k_source.1, s32[]{:T(128)S(6)} %select_n.38, s32[]{:T(128)S(6)} %select_n.37), kind=kLoop, calls=%fused_computation.9 | loop fusion | bytes 4194312 | tf_op jit(solution)/shard_map/dynamic_slice | solution.py:322
  4.8 0.3 collective-permute-start.1
  5.1 2.9 %collective-permute-start.3 = (bf16[16,4608]{1,0:T(8,128)(2,1)S(1)}, bf16[16,4608]{1,0:T(8,128)(2,1)S(1)}, u32[]{:S(2)}, u32[]{:S(2)}) collective-permute-start(bf16[16,4608]{1,0:T(8,128)(2,1)S(1)} %maximum_maximum_fusion.refs_0_.refs_7_), channel_id=1, source_target_pairs={{0,2},{1,3},{2,0},{3,1},{4,6},{5,7},{6,4},{7,5},{8,10},{9,11},{10,... | collective-permute-start | bytes 442376 | tf_op jit(solution)/shard_map/ppermute | solution.py:319
  8.0 1.6 %collective-permute-start.4 = (bf16[16,4608]{1,0:T(8,128)(2,1)S(1)}, bf16[16,4608]{1,0:T(8,128)(2,1)S(1)}, u32[]{:S(2)}, u32[]{:S(2)}) collective-permute-start(bf16[16,4608]{1,0:T(8,128)(2,1)S(1)} %maximum_maximum_fusion.refs_0_.refs_7_), channel_id=1, source_target_pairs={{0,4},{1,5},{2,6},{3,7},{4,0},{5,1},{6,2},{7,3},{8,12},{9,13},{10,... | collective-permute-start | bytes 442376 | tf_op jit(solution)/shard_map/ppermute | solution.py:319
  9.5 2.6 %collective-permute-start.6 = (bf16[16,4608]{1,0:T(8,128)(2,1)S(1)}, bf16[16,4608]{1,0:T(8,128)(2,1)S(1)}, u32[]{:S(2)}, u32[]{:S(2)}) collective-permute-start(bf16[16,4608]{1,0:T(8,128)(2,1)S(1)} %maximum_maximum_fusion.refs_0_.refs_7_), channel_id=1, source_target_pairs={{0,8},{1,9},{2,10},{3,11},{4,12},{5,13},{6,14},{7,15},{8,0},{9,1},... | collective-permute-start | bytes 442376 | tf_op jit(solution)/shard_map/ppermute | solution.py:319
  12.1 0.0 copy-done.2
  12.8 0.1 pad.6.clone
  12.9 0.0 collective-permute-done.3.refs_1_.refs_8_
  12.9 3.6 %collective-permute-done.4.refs_2_.refs_9_ = bf16[16,4608]{1,0:T(8,128)(2,1)S(1)} collective-permute-done((bf16[16,4608]{1,0:T(8,128)(2,1)S(1)}, bf16[16,4608]{1,0:T(8,128)(2,1)S(1)}, u32[]{:S(2)}, u32[]{:S(2)}) %collective-permute-start.4) | collective-permute-done | bytes 147488 | tf_op jit(solution)/shard_map/ppermute | solution.py:319
  16.4 2.6 %collective-permute-done.6.refs_0_.refs_11_ = bf16[16,4608]{1,0:T(8,128)(2,1)S(1)} collective-permute-done((bf16[16,4608]{1,0:T(8,128)(2,1)S(1)}, bf16[16,4608]{1,0:T(8,128)(2,1)S(1)}, u32[]{:S(2)}, u32[]{:S(2)}) %collective-permute-start.6) | collective-permute-done | bytes 147488 | tf_op jit(solution)/shard_map/ppermute | solution.py:319
  19.0 0.4 collective-permute-start.8
  19.5 0.0 copy-done.3
  19.5 0.5 collective-permute-start.5
  20.0 1.5 %collective-permute-start.7 = (bf16[16,4608]{1,0:T(8,128)(2,1)S(1)}, bf16[16,4608]{1,0:T(8,128)(2,1)S(1)}, u32[]{:S(2)}, u32[]{:S(2)}) collective-permute-start(bf16[16,4608]{1,0:T(8,128)(2,1)S(1)} %collective-permute-done.6.refs_0_.refs_11_), channel_id=1, source_target_pairs={{0,2},{1,3},{2,0},{3,1},{4,6},{5,7},{6,4},{7,5},{8,10},{9,11},{10,... | collective-permute-start | bytes 442376 | tf_op jit(solution)/shard_map/ppermute | solution.py:319
  21.5 0.1 add_add_fusion.own_ref
  21.6 0.0 collective-permute-start.9
  21.6 1.2 %collective-permute-done.9.sib_ref = s32[3,640]{1,0:T(4,128)S(1)} collective-permute-done((s32[3,640]{1,0:T(4,128)S(1)}, s32[3,640]{1,0:T(4,128)S(1)}, u32[]{:S(2)}, u32[]{:S(2)}) %collective-permute-start.9) | collective-permute-done | bytes 7712 | tf_op jit(solution)/shard_map/ppermute | solution.py:319
  22.8 1.3 %codes.1 = (f32[8,640]{1,0:T(8,128)S(1)}, f32[8,640]{1,0:T(8,128)S(1)}, f32[640,8]{1,0:T(8,128)S(1)}) custom-call(s32[3,640]{1,0:T(4,128)S(1)} %add_add_fusion.own_ref, s32[3,640]{1,0:T(4,128)S(1)} %collective-permute-done.9.sib_ref), custom_call_target="tpu_custom_call" | custom-call | tf_op jit(solution)/shard_map/codes/pallas_call | solution.py:400
  24.1 0.7 copy-done
  24.8 0.7 collective-permute-done.5.refs_3_.refs_10_
  25.6 0.0 collective-permute-done.8.refs_5_.refs_13_
  25.6 0.5 collective-permute-start.10
  26.1 1.1 %collective-permute-done.7.refs_1_.refs_12_ = bf16[16,4608]{1,0:T(8,128)(2,1)S(1)} collective-permute-done((bf16[16,4608]{1,0:T(8,128)(2,1)S(1)}, bf16[16,4608]{1,0:T(8,128)(2,1)S(1)}, u32[]{:S(2)}, u32[]{:S(2)}) %collective-permute-start.7) | collective-permute-done | bytes 147488 | tf_op jit(solution)/shard_map/ppermute | solution.py:319
  27.1 0.0 collective-permute-done.1.refs_5_.refs_3_.refs_2_
  27.1 10.0 %early_stats.3.refs_4_ = f32[2,4,128]{2,1,0:T(4,128)S(1)} custom-call(bf16[16,4608]{1,0:T(8,128)(2,1)S(1)} %collective-permute-done.6.refs_0_.refs_11_, bf16[16,4608]{1,0:T(8,128)(2,1)S(1)} %collective-permute-done.7.refs_1_.refs_12_, bf16[1024,512]{1,0:T(8,128)(2,1)S(1)} %get-tuple-element.26.refs_4_.refs_2_.refs_1_, ...), custom_call_target="tpu_custom_call" | custom-call | flops 536870912 | bytes 1048576 | tf_op jit(solution)/shard_map/early_stats/pallas_call | solution.py:362
  37.2 2.5 %early_stats.2.refs_3_ = f32[4,4,128]{2,1,0:T(4,128)S(1)} custom-call(bf16[16,4608]{1,0:T(8,128)(2,1)S(1)} %maximum_maximum_fusion.refs_0_.refs_7_, bf16[16,4608]{1,0:T(8,128)(2,1)S(1)} %collective-permute-done.3.refs_1_.refs_8_, bf16[16,4608]{1,0:T(8,128)(2,1)S(1)} %collective-permute-done.4.refs_2_.refs_9_, ...), custom_call_target="tpu_custom_call" | custom-call | flops 1073741824 | bytes 1048576 | tf_op jit(solution)/shard_map/early_stats/pallas_call | solution.py:362
  39.7 0.0 collective-permute-done.10.refs_6_.refs_14_
  39.7 2.1 %late_stats.1 = f32[8,8,4,128]{3,2,1,0:T(4,128)} custom-call(s32[1]{0:T(128)} %bitcast.refs_0_, bf16[1024,512]{1,0:T(8,128)(2,1)S(1)} %get-tuple-element.26.refs_4_.refs_2_.refs_1_, bf16[1024,512]{1,0:T(8,128)(2,1)S(1)} %collective-permute-done.1.refs_5_.refs_3_.refs_2_, f32[4,4,128]{2,1,0:T(4,128)S(1)} %early_stats.2.refs_3_, ...), custom_call_target="tpu_custom_call" | custom-call | flops 536870912 | bytes 1048576 | tf_op jit(solution)/shard_map/late_stats/pallas_call | solution.py:424
  41.8 6.3 %all-to-all-start = ((f32[8,8,4,128]{3,2,1,0:T(4,128)}), f32[8,8,4,128]{3,2,1,0:T(4,128)S(1)}, u32[]{:S(2)}, u32[]{:S(2)}) async-start(f32[8,8,4,128]{3,2,1,0:T(4,128)} %late_stats.1), calls=%async_computation | async-start | bytes 262144 | tf_op jit(solution)/shard_map/all_to_all | solution.py:456
  48.1 6.4 %compact.1.refs_6_ = bf16[16,48,256]{2,1,0:T(8,128)(2,1)} custom-call(f32[640,8]{1,0:T(8,128)} %copy-done, bf16[1024,1024]{1,0:T(8,128)(2,1)} %k_source.1, bf16[1024,1024]{1,0:T(8,128)(2,1)} %v_source.1), custom_call_target="tpu_custom_call" | custom-call | flops 2684354560 | bytes 4194304 | tf_op jit(solution)/shard_map/compact/pallas_call | solution.py:437
  54.5 0.9 all-to-all-done.refs_1_
  55.4 1.0 %copy-done.1 = bf16[16,48,256]{2,1,0:T(8,128)(2,1)S(1)} copy-done((bf16[16,48,256]{2,1,0:T(8,128)(2,1)S(1)}, bf16[16,48,256]{2,1,0:T(8,128)(2,1)}, u32[]{:S(2)}) %copy-start.1) | copy-done | bytes 393240
  56.4 7.1 %mass.1 = (f32[4,1024]{1,0:T(4,128)S(1)}, f32[4,1024]{1,0:T(4,128)S(1)}, bf16[16,48,256]{2,1,0:T(8,128)(2,1)}) custom-call(s32[1]{0:T(128)} %bitcast.refs_0_, f32[8,8,4,128]{3,2,1,0:T(4,128)S(1)} %all-to-all-done.refs_1_, bf16[1024,512]{1,0:T(8,128)(2,1)S(1)} %get-tuple-element.26.refs_4_.refs_2_.refs_1_, ...), custom_call_target="tpu_custom_call" | custom-call | flops 2147483648 | bytes 1048576 | tf_op jit(solution)/shard_map/mass/pallas_call | solution.py:465
  63.5 20.5 %all-to-all-start.1 = ((bf16[16,48,256]{2,1,0:T(8,128)(2,1)}), bf16[16,48,256]{2,1,0:T(8,128)(2,1)S(1)}, u32[]{:S(2)}, u32[]{:S(2)}) async-start(bf16[16,48,256]{2,1,0:T(8,128)(2,1)} %get-tuple-element.24), calls=%async_computation.1 | async-start | bytes 786432 | tf_op jit(solution)/shard_map/all_to_all | solution.py:484
  84.0 0.4 collective-permute-start.11
  84.4 0.8 collective-permute-done.11
  85.3 0.6 maximum_select_fusion
  85.9 10.3 %all-to-all-done.1 = bf16[16,48,256]{2,1,0:T(8,128)(2,1)S(1)} async-done(((bf16[16,48,256]{2,1,0:T(8,128)(2,1)}), bf16[16,48,256]{2,1,0:T(8,128)(2,1)S(1)}, u32[]{:S(2)}, u32[]{:S(2)}) %all-to-all-start.1) | async-done | bytes 393248 | tf_op jit(solution)/shard_map/all_to_all | solution.py:484
  96.2 0.7 add.28
  96.9 0.7 slice.24
  (10 shorter events, 0.0 us)
Async XLA Ops:
  0.6 2.5 %collective-permute-start = (bf16[8,8192]{1,0:T(8,128)(2,1)}, bf16[8,8192]{1,0:T(8,128)(2,1)S(1)}, u32[]{:S(2)}, u32[]{:S(2)}) collective-permute-start(bf16[8,8192]{1,0:T(8,128)(2,1)} %param.8), channel_id=1, source_target_pairs={{0,1},{1,0},{2,3},{3,2},{4,5},{5,4},{6,7},{7,6},{8,9},{9,8},{10,11... | collective-permute-start | bytes 393224 | tf_op jit(solution)/shard_map/ppermute | solution.py:319
  1.9 1.2 %collective-permute-start.2 = (bf16[8,1024]{1,0:T(8,128)(2,1)S(1)}, bf16[8,1024]{1,0:T(8,128)(2,1)S(1)}, u32[]{:S(2)}, u32[]{:S(2)}) collective-permute-start(bf16[8,1024]{1,0:T(8,128)(2,1)S(1)} %slice_select_fusion), channel_id=1, source_target_pairs={{0,1},{1,0},{2,3},{3,2},{4,5},{5,4},{6,7},{7,6},{8,9},{9,8},{10,11... | collective-permute-start | bytes 49160 | tf_op jit(solution)/shard_map/ppermute | solution.py:319
  3.1 9.1 %copy-start.2 = (s32[640]{0:T(1024)S(1)}, s32[640]{0:T(1024)}, u32[]{:S(2)}) copy-start(s32[640]{0:T(1024)} %param.11) | copy-start | bytes 7684
  3.1 16.4 %copy-start.3 = (s32[640]{0:T(1024)S(1)}, s32[640]{0:T(1024)}, u32[]{:S(2)}) copy-start(s32[640]{0:T(1024)} %param.10) | copy-start | bytes 7684
  4.8 22.4 %collective-permute-start.1 = (bf16[1024,512]{1,0:T(8,128)(2,1)S(1)}, bf16[1024,512]{1,0:T(8,128)(2,1)S(1)}, u32[]{:S(2)}, u32[]{:S(2)}) collective-permute-start(bf16[1024,512]{1,0:T(8,128)(2,1)S(1)} %get-tuple-element.25), channel_id=1, source_target_pairs={{0,1},{1,0},{2,3},{3,2},{4,5},{5,4},{6,7},{7,6},{8,9},{9,8},{10,11... | collective-permute-start | bytes 3145736 | tf_op jit(solution)/shard_map/ppermute | solution.py:319
  5.1 7.8 %collective-permute-start.3 = (bf16[16,4608]{1,0:T(8,128)(2,1)S(1)}, bf16[16,4608]{1,0:T(8,128)(2,1)S(1)}, u32[]{:S(2)}, u32[]{:S(2)}) collective-permute-start(bf16[16,4608]{1,0:T(8,128)(2,1)S(1)} %maximum_maximum_fusion.refs_0_.refs_7_), channel_id=1, source_target_pairs={{0,2},{1,3},{2,0},{3,1},{4,6},{5,7},{6,4},{7,5},{8,10},{9,11},{10,... | collective-permute-start | bytes 442376 | tf_op jit(solution)/shard_map/ppermute | solution.py:319
  8.0 8.5 %collective-permute-start.4 = (bf16[16,4608]{1,0:T(8,128)(2,1)S(1)}, bf16[16,4608]{1,0:T(8,128)(2,1)S(1)}, u32[]{:S(2)}, u32[]{:S(2)}) collective-permute-start(bf16[16,4608]{1,0:T(8,128)(2,1)S(1)} %maximum_maximum_fusion.refs_0_.refs_7_), channel_id=1, source_target_pairs={{0,4},{1,5},{2,6},{3,7},{4,0},{5,1},{6,2},{7,3},{8,12},{9,13},{10,... | collective-permute-start | bytes 442376 | tf_op jit(solution)/shard_map/ppermute | solution.py:319
  9.5 9.5 %collective-permute-start.6 = (bf16[16,4608]{1,0:T(8,128)(2,1)S(1)}, bf16[16,4608]{1,0:T(8,128)(2,1)S(1)}, u32[]{:S(2)}, u32[]{:S(2)}) collective-permute-start(bf16[16,4608]{1,0:T(8,128)(2,1)S(1)} %maximum_maximum_fusion.refs_0_.refs_7_), channel_id=1, source_target_pairs={{0,8},{1,9},{2,10},{3,11},{4,12},{5,13},{6,14},{7,15},{8,0},{9,1},... | collective-permute-start | bytes 442376 | tf_op jit(solution)/shard_map/ppermute | solution.py:319
  19.0 6.5 %collective-permute-start.8 = (bf16[16,4608]{1,0:T(8,128)(2,1)S(1)}, bf16[16,4608]{1,0:T(8,128)(2,1)S(1)}, u32[]{:S(2)}, u32[]{:S(2)}) collective-permute-start(bf16[16,4608]{1,0:T(8,128)(2,1)S(1)} %collective-permute-done.6.refs_0_.refs_11_), channel_id=1, source_target_pairs={{0,4},{1,5},{2,6},{3,7},{4,0},{5,1},{6,2},{7,3},{8,12},{9,13},{10,... | collective-permute-start | bytes 442376 | tf_op jit(solution)/shard_map/ppermute | solution.py:319
  19.5 6.1 %collective-permute-start.5 = (bf16[16,4608]{1,0:T(8,128)(2,1)S(1)}, bf16[16,4608]{1,0:T(8,128)(2,1)S(1)}, u32[]{:S(2)}, u32[]{:S(2)}) collective-permute-start(bf16[16,4608]{1,0:T(8,128)(2,1)S(1)} %collective-permute-done.4.refs_2_.refs_9_), channel_id=1, source_target_pairs={{0,2},{1,3},{2,0},{3,1},{4,6},{5,7},{6,4},{7,5},{8,10},{9,11},{10,... | collective-permute-start | bytes 442376 | tf_op jit(solution)/shard_map/ppermute | solution.py:319
  20.0 7.1 %collective-permute-start.7 = (bf16[16,4608]{1,0:T(8,128)(2,1)S(1)}, bf16[16,4608]{1,0:T(8,128)(2,1)S(1)}, u32[]{:S(2)}, u32[]{:S(2)}) collective-permute-start(bf16[16,4608]{1,0:T(8,128)(2,1)S(1)} %collective-permute-done.6.refs_0_.refs_11_), channel_id=1, source_target_pairs={{0,2},{1,3},{2,0},{3,1},{4,6},{5,7},{6,4},{7,5},{8,10},{9,11},{10,... | collective-permute-start | bytes 442376 | tf_op jit(solution)/shard_map/ppermute | solution.py:319
  21.6 1.2 %collective-permute-start.9 = (s32[3,640]{1,0:T(4,128)S(1)}, s32[3,640]{1,0:T(4,128)S(1)}, u32[]{:S(2)}, u32[]{:S(2)}) collective-permute-start(s32[3,640]{1,0:T(4,128)S(1)} %add_add_fusion.own_ref), channel_id=1, source_target_pairs={{0,1},{1,0},{2,3},{3,2},{4,5},{5,4},{6,7},{7,6},{8,9},{9,8},{10,11... | collective-permute-start | bytes 23048 | tf_op jit(solution)/shard_map/ppermute | solution.py:319
  24.1 0.7 copy-start
  25.6 14.1 %collective-permute-start.10 = (bf16[16,4608]{1,0:T(8,128)(2,1)S(1)}, bf16[16,4608]{1,0:T(8,128)(2,1)S(1)}, u32[]{:S(2)}, u32[]{:S(2)}) collective-permute-start(bf16[16,4608]{1,0:T(8,128)(2,1)S(1)} %collective-permute-done.8.refs_5_.refs_13_), channel_id=1, source_target_pairs={{0,2},{1,3},{2,0},{3,1},{4,6},{5,7},{6,4},{7,5},{8,10},{9,11},{10,... | collective-permute-start | bytes 442376 | tf_op jit(solution)/shard_map/ppermute | solution.py:319
  41.8 13.6 %all-to-all-start = ((f32[8,8,4,128]{3,2,1,0:T(4,128)}), f32[8,8,4,128]{3,2,1,0:T(4,128)S(1)}, u32[]{:S(2)}, u32[]{:S(2)}) async-start(f32[8,8,4,128]{3,2,1,0:T(4,128)} %late_stats.1), calls=%async_computation | async-start | bytes 262144 | tf_op jit(solution)/shard_map/all_to_all | solution.py:456
  55.4 1.0 %copy-start.1 = (bf16[16,48,256]{2,1,0:T(8,128)(2,1)S(1)}, bf16[16,48,256]{2,1,0:T(8,128)(2,1)}, u32[]{:S(2)}) copy-start(bf16[16,48,256]{2,1,0:T(8,128)(2,1)} %compact.1.refs_6_) | copy-start | bytes 1179652
  63.5 32.7 %all-to-all-start.1 = ((bf16[16,48,256]{2,1,0:T(8,128)(2,1)}), bf16[16,48,256]{2,1,0:T(8,128)(2,1)S(1)}, u32[]{:S(2)}, u32[]{:S(2)}) async-start(bf16[16,48,256]{2,1,0:T(8,128)(2,1)} %get-tuple-element.24), calls=%async_computation.1 | async-start | bytes 786432 | tf_op jit(solution)/shard_map/all_to_all | solution.py:484
  84.0 1.2 %collective-permute-start.11 = (f32[4,1024]{1,0:T(4,128)S(1)}, f32[4,1024]{1,0:T(4,128)S(1)}, u32[]{:S(2)}, u32[]{:S(2)}) collective-permute-start(f32[4,1024]{1,0:T(4,128)S(1)} %get-tuple-element.23), channel_id=1, source_target_pairs={{0,1},{1,0},{2,3},{3,2},{4,5},{5,4},{6,7},{7,6},{8,9},{9,8},{10,11... | collective-permute-start | bytes 49160 | tf_op jit(solution)/shard_map/ppermute | solution.py:319
